TPU v7x, 256 devices: a whole 4x4x8 slice. The times are simulated.
256 devices in a mesh: days: 8 (over z), row: 2 (over core), col: 16 (over x, y).
Axes of the slice: x: 4, y: 4, z: 8, core: 2. Of those that a mesh axis runs over, the one named last changes fastest.
Arguments:
- inverse_blocks: bfloat16 [16, 1024, 1024], P('days', 'col', 'row'), may hold values from -1 to 1, as said below
- factor_blocks: bfloat16 [16, 1024, 1024], P('days', 'col', 'row'), may hold values from -1.1 to 1.1
- sigma_end: bfloat16 [1024, 1024], P('col', 'row'), may hold values from -5 to 5, as said below
Outputs:
- marginal_covariance: bfloat16 [16, 1024, 1024], P('days', 'col', 'row')
- cross_covariance: bfloat16 [16, 1024, 1024], P('days', 'col', 'row')
Inputs may be any that keep to these rules, and one draw needn't show every extreme that they name: `inverse_blocks`: each day's block is symmetric. `sigma_end`: symmetric.
All inputs are finite; a program needn't handle non-finite values.
Results may differ from a plain program's by a relative error of at most 0.0025.
The roundings to bfloat16 on the way count: a program that leaves them out, or rounds other values in their place, can miss the bound.
Values may be sent and summed in bfloat16 or wider, within the bound.
No kernel may reach another device: no remote copies, remote signals or barrier semaphores. Data moves between devices by JAX's collectives and lax.ppermute only.
A program may use at most 64 MiB of HBM per device.

v0:
```python
import jax
import jax.numpy as jnp
from jax import lax
from jax.experimental import pallas as pl
from jax.experimental.pallas import tpu as pltpu
from jax.sharding import PartitionSpec as P

narrow = jnp.bfloat16
wide = jnp.float32
STRIP = 32
PACK = 8
VMEM_LIMIT = 20 * 1024 * 1024


def shifted(value, steps, sources=None):
    count = lax.axis_size("days")
    sources = range(steps, count) if sources is None else sources
    return lax.ppermute(value, "days", [(source, source - steps) for source in sources])


def other_core(value):
    return lax.ppermute(value, "row", [(0, 1), (1, 0)])


def ordered(own, other, axis):
    first = lax.axis_index("row") == 0
    return jnp.concatenate([jnp.where(first, own, other), jnp.where(first, other, own)], axis=axis)


def both_cores(value, axis):
    return ordered(value, other_core(value), axis)


def spread(value):
    count = lax.axis_size("col")
    return lax.all_to_all(
        jnp.broadcast_to(value[None], (count,) + value.shape), "col", 0, 0, tiled=True
    )


def halves(value):
    high = value.astype(narrow)
    return (high, (value - high.astype(wide)).astype(narrow))


def times(pieces, factor_ref, day):
    _, chips, rows, nodes = factor_ref.shape
    return jnp.dot(
        pieces, factor_ref[day].reshape(chips * rows, nodes), preferred_element_type=wide
    )


def times_wide(rows, factor_ref, day):
    split = times(jnp.concatenate(halves(rows), 0), factor_ref, day)
    count = rows.shape[0]
    return split[:count] + split[count:]


def pack(rows, out_ref, place):
    devices = out_ref.shape[0]
    chips = devices // 2
    padded = jnp.concatenate([rows, jnp.zeros((128 - STRIP, rows.shape[1]), wide)], axis=0)
    turned = padded.T
    for core in range(2):
        for chip in range(chips):
            start = (2 * chip + core) * STRIP
            for part in range(STRIP // PACK):
                out_ref[
                    core * chips + chip,
                    place * PACK : (place + 1) * PACK,
                    part * STRIP : (part + 1) * STRIP,
                ] = turned[start + part * PACK : start + (part + 1) * PACK, :STRIP]


def unpack(in_ref, place, rows_ref):
    devices = in_ref.shape[0]
    chips = devices // 2
    for core in range(2):
        for chip in range(chips):
            start = (2 * chip + core) * STRIP
            for part in range(STRIP // PACK):
                rows_ref[part * PACK : (part + 1) * PACK, start : start + STRIP] = in_ref[
                    core * chips + chip,
                    place * PACK : (place + 1) * PACK,
                    part * STRIP : (part + 1) * STRIP,
                ]


def stage(own_ref, other_ref, out_ref, sems):
    core = lax.axis_index("row")
    days, _, _, nodes = out_ref.shape
    half = nodes // 2
    copies = []
    for day in range(days):
        for which, (ref, place) in enumerate(((own_ref, core), (other_ref, 1 - core))):
            start = pl.multiple_of(place * half, half)
            copies.append(
                pltpu.make_async_copy(
                    ref.at[:, day],
                    out_ref.at[day, :, :, pl.ds(start, half)],
                    sems.at[2 * day + which],
                )
            )
    for copy in copies:
        copy.start()
    for copy in copies:
        copy.wait()


def staged(own, other):
    chips, days, rows, half = own.shape
    return pl.pallas_call(
        stage,
        out_shape=pltpu.VMEM((days, chips, rows, 2 * half), narrow),
        in_specs=[pl.BlockSpec(memory_space=pl.ANY)] * 2,
        out_specs=pl.BlockSpec(memory_space=pltpu.VMEM),
        scratch_shapes=[pltpu.SemaphoreType.DMA((2 * days,))],
        compiler_params=pltpu.CompilerParams(vmem_limit_bytes=VMEM_LIMIT),
    )(own, other)


def first_out(inverse_ref, sigma_ref, factor_ref, out_ref):
    later = times(sigma_ref[...], factor_ref, 1)
    stacked = jnp.concatenate([inverse_ref[...], *halves(later)], 0)
    split = times(stacked, factor_ref, 0)
    pack(split[:STRIP], out_ref, 0)
    pack(split[STRIP : 2 * STRIP] + split[2 * STRIP :], out_ref, 1)


def first_in(packed_ref, base_ref, factor_ref, out_ref, near_ref, far_ref):
    unpack(packed_ref, 0, near_ref)
    unpack(packed_ref, 1, far_ref)
    later = near_ref[...] + times_wide(far_ref[...], factor_ref, 1)
    out_ref[...] = base_ref[...].astype(wide) + times_wide(later, factor_ref, 0)


def all_days(rows, factor_refs):
    for ref in factor_refs:
        for day in (1, 0):
            rows = times_wide(rows, ref, day)
    return rows


def step_out(rows_ref, *refs):
    pack(all_days(rows_ref[...], refs[:-1]), refs[-1], 0)


def step_in(packed_ref, base_ref, *refs):
    out_ref, rows_ref = refs[-2:]
    unpack(packed_ref, 0, rows_ref)
    out_ref[...] = base_ref[...] + all_days(rows_ref[...], refs[:-2])


def call(body, shape, scratch, operands, factors):
    vmem = pl.BlockSpec(memory_space=pltpu.VMEM)
    factors = [pltpu.with_memory_space_constraint(factor, pltpu.VMEM) for factor in factors]
    return pl.pallas_call(
        body,
        out_shape=jax.ShapeDtypeStruct(shape, wide),
        in_specs=[vmem] * (len(operands) + len(factors)),
        out_specs=vmem,
        scratch_shapes=[pltpu.VMEM(size, wide) for size in scratch],
        compiler_params=pltpu.CompilerParams(vmem_limit_bytes=VMEM_LIMIT),
    )(*operands, *factors)


def traded(value):
    return lax.all_to_all(value, ("row", "col"), 0, 0, tiled=True)


def product(left, right):
    return jnp.dot(left, right, preferred_element_type=wide)


def product_t(left, right):
    return lax.dot_general(left, right, (((0,), (0,)), ((), ())), preferred_element_type=wide)


def shards(inverse_blocks, factor_blocks, sigma_end):
    chips = lax.axis_size("col")
    days, rows, half = factor_blocks.shape
    nodes = chips * rows
    devices = 2 * chips
    core = lax.axis_index("row")
    chip = lax.axis_index("col")
    group = lax.axis_index("days")
    final_group = group == lax.axis_size("days") - 1

    fixed = jnp.stack([inverse_blocks[0], inverse_blocks[1], sigma_end])
    ahead, fixed_other = lax.optimization_barrier(
        (shifted(factor_blocks, 1), other_core(fixed))
    )
    next_mine = lax.all_gather(ahead, "col", axis=0)
    fixed = ordered(fixed, fixed_other, 2)
    mine = spread(factor_blocks)
    own = staged(mine, other_core(mine))

    strips = lax.dynamic_slice_in_dim(fixed, core * STRIP, STRIP, 1)
    base, last_strip, sigma_strip = (strips[0], strips[1], strips[2])
    started = jnp.where(final_group, sigma_strip, jnp.zeros_like(sigma_strip))

    strip_shape = (STRIP, nodes)
    packed = call(first_out, (devices, 2 * PACK, 128), [], [last_strip, started], [own])
    first_state = call(first_in, strip_shape, [strip_shape] * 2, [traded(packed), base], [own])

    def step(base, arrived, factors):
        packed = call(step_out, (devices, PACK, 128), [], [arrived], factors)
        return call(step_in, strip_shape, [strip_shape], [traded(packed), base], factors)

    even = range(2, lax.axis_size("days"), 2)
    state = step(first_state, shifted(first_state, 1), [own])
    pair_state, next_mine = lax.optimization_barrier((state, next_mine))
    following = staged(next_mine, other_core(next_mine))
    inverse_last = lax.all_gather(inverse_blocks[1], "col", axis=0)
    state = step(pair_state, shifted(pair_state, 2, even), [following, own])
    state = step(pair_state, shifted(state, 2, even), [following, own])
    state, inverse_last = lax.optimization_barrier((state, inverse_last))
    inverse_last_full = both_cores(inverse_last, 2).reshape(nodes, nodes)
    beside = shifted(state.astype(narrow), 1, even)
    state = step(shifted(first_state, 1), shifted(state, 2, even), [following])

    separator = jnp.where(group % 2 == 0, state.astype(narrow), beside)
    separator = jnp.where(final_group, sigma_strip, separator)
    strips = spread(separator)
    covariance = ordered(strips, other_core(strips), 1).reshape(nodes, nodes)

    factor_first, factor_last = (own[0].reshape(nodes, nodes), own[1].reshape(nodes, nodes))
    cross_last = product(covariance, factor_last).astype(narrow)
    marginal_last = (
        inverse_last_full.astype(wide) + product_t(factor_last, cross_last)
    ).astype(narrow)
    factor_first_half = mine[:, 0].reshape(nodes, half)
    cross_first_half = product(marginal_last, factor_first_half).astype(narrow)
    factor_first_rows = lax.dynamic_slice_in_dim(factor_first, chip * rows, rows, 1)
    marginal_first = (
        inverse_blocks[0].astype(wide) + product_t(factor_first_rows, cross_first_half)
    ).astype(narrow)

    def mine_of(value):
        return lax.dynamic_slice(value, (chip * rows, core * half), (rows, half))

    cross_first = lax.dynamic_slice_in_dim(cross_first_half, chip * rows, rows, 0)
    return (
        jnp.stack([marginal_first, mine_of(marginal_last)]),
        jnp.stack([cross_first, mine_of(cross_last)]),
    )


def solution(mesh):
    placed = (P("days", "col", "row"), P("days", "col", "row"), P("col", "row"))
    return jax.shard_map(
        shards,
        mesh=mesh,
        in_specs=placed,
        out_specs=(P("days", "col", "row"), P("days", "col", "row")),
        check_vma=False,
    )
```

profile of v0, /device:TPU:1, one launch (start us, length us, event | category | flops | bytes accessed | tf_op | source)
XLA Modules:
  0.0 213.4 jit_solution(17498220618475089109)
XLA Ops:
  7.2 2.5 %broadcast_in_dim.6 = bf16[16,2,64,512]{3,2,1,0:T(8,128)(2,1)} broadcast(bf16[2,64,512]{2,1,0:T(8,128)(2,1)} %param.4), dimensions={1,2,3} | broadcast | bytes 2228224 | tf_op jit(solution)/shard_map/broadcast_in_dim | solution.py:37
  9.7 7.7 %all-to-all-start = ((bf16[16,2,64,512]{3,2,1,0:T(8,128)(2,1)}), bf16[16,2,64,512]{3,2,1,0:T(8,128)(2,1)S(1)}, u32[]{:S(2)}, u32[]{:S(2)}) async-start(bf16[16,2,64,512]{3,2,1,0:T(8,128)(2,1)} %broadcast_in_dim.6), calls=%async_computation | async-start | bytes 4194304 | tf_op jit(solution)/shard_map/all_to_all | solution.py:36
  17.4 0.0 all-gather.6.cloned.1.call-start
  17.5 1.0 collective-permute-start.2
  18.5 1.3 collective-permute-start.1
  19.8 6.0 %collective-permute-done.1 = bf16[2,64,512]{2,1,0:T(8,128)(2,1)S(1)} collective-permute-done((bf16[2,64,512]{2,1,0:T(8,128)(2,1)S(1)}, bf16[2,64,512]{2,1,0:T(8,128)(2,1)S(1)}, u32[]{:S(2)}, u32[]{:S(2)}) %collective-permute-start.1) | collective-permute-done | bytes 131104 | tf_op jit(solution)/shard_map/ppermute | solution.py:18
  25.8 0.7 copy-done.10
  26.5 0.0 all-gather.6.cloned.1.call-update
  26.5 0.0 all-gather.4.cloned.1.call-start
  26.5 18.7 %all-to-all-done.own_ref = bf16[16,2,64,512]{3,2,1,0:T(8,128)(2,1)S(1)} async-done(((bf16[16,2,64,512]{3,2,1,0:T(8,128)(2,1)}), bf16[16,2,64,512]{3,2,1,0:T(8,128)(2,1)S(1)}, u32[]{:S(2)}, u32[]{:S(2)}) %all-to-all-start) | async-done | bytes 2097184 | tf_op jit(solution)/shard_map/all_to_all | solution.py:36
  45.3 3.6 %collective-permute-start = (bf16[16,2,64,512]{3,2,1,0:T(8,128)(2,1)S(1)}, bf16[16,2,64,512]{3,2,1,0:T(8,128)(2,1)}, u32[]{:S(2)}, u32[]{:S(2)}) collective-permute-start(bf16[16,2,64,512]{3,2,1,0:T(8,128)(2,1)S(1)} %all-to-all-done.own_ref), channel_id=1, source_target_pairs={{0,16},{16,0},{1,17},{17,1},{2,18},{18,2},{3,19},{19,3},{4,20},{20... | collective-permute-start | bytes 6291464 | tf_op jit(solution)/shard_map/ppermute | solution.py:22
  48.9 3.8 %collective-permute-done.other_ref = bf16[16,2,64,512]{3,2,1,0:T(8,128)(2,1)} collective-permute-done((bf16[16,2,64,512]{3,2,1,0:T(8,128)(2,1)S(1)}, bf16[16,2,64,512]{3,2,1,0:T(8,128)(2,1)}, u32[]{:S(2)}, u32[]{:S(2)}) %collective-permute-start) | collective-permute-done | bytes 2097184 | tf_op jit(solution)/shard_map/ppermute | solution.py:22
  52.8 1.8 shard_map.50.factor_ref.refs_0_.refs_1_
  54.6 1.3 shard_map.51
  55.8 12.6 %all_to_all.35.packed_ref = f32[32,16,128]{2,1,0:T(8,128)S(1)} all-to-all(f32[32,16,128]{2,1,0:T(8,128)S(1)} %shard_map.51), channel_id=1, replica_groups=mesh['days'=8,'row'=2,'col'=16] {'row','col'}, dimensions={0} | all-to-all | bytes 524288 | tf_op jit(solution)/shard_map/all_to_all | solution.py:168
  68.4 0.9 shard_map.52.base_ref
  69.3 1.3 collective-permute-start.3
  70.6 5.5 %collective-permute-done.3.rows_ref.base_ref = f32[32,1024]{1,0:T(8,128)S(1)} collective-permute-done((f32[32,1024]{1,0:T(8,128)S(1)}, f32[32,1024]{1,0:T(8,128)S(1)}, u32[]{:S(2)}, u32[]{:S(2)}) %collective-permute-start.3) | collective-permute-done | bytes 131104 | tf_op jit(solution)/shard_map/ppermute | solution.py:18
  76.1 1.1 shard_map.53
  77.2 12.0 %all_to_all.36.packed_ref = f32[32,8,128]{2,1,0:T(8,128)S(1)} all-to-all(f32[32,8,128]{2,1,0:T(8,128)S(1)} %shard_map.53), channel_id=1, replica_groups=mesh['days'=8,'row'=2,'col'=16] {'row','col'}, dimensions={0} | all-to-all | bytes 262144 | tf_op jit(solution)/shard_map/all_to_all | solution.py:168
  89.2 0.9 shard_map.54.base_ref
  90.1 0.0 all-gather.6.cloned.1.call-done
  90.1 0.7 collective-permute-start.5
  90.8 0.6 slice.32
  91.5 1.6 collective-permute-start.4
  93.0 1.9 collective-permute-done.5.other_ref
  94.9 1.6 copy-done.5
  96.5 1.8 shard_map.55.refs_0_
  98.3 2.2 %collective-permute-done.4.rows_ref = f32[32,1024]{1,0:T(8,128)S(1)} collective-permute-done((f32[32,1024]{1,0:T(8,128)S(1)}, f32[32,1024]{1,0:T(8,128)S(1)}, u32[]{:S(2)}, u32[]{:S(2)}) %collective-permute-start.4) | collective-permute-done | bytes 131104 | tf_op jit(solution)/shard_map/ppermute | solution.py:18
  100.5 1.8 shard_map.56
  102.3 11.5 %all_to_all.37.packed_ref = f32[32,8,128]{2,1,0:T(8,128)S(1)} all-to-all(f32[32,8,128]{2,1,0:T(8,128)S(1)} %shard_map.56), channel_id=1, replica_groups=mesh['days'=8,'row'=2,'col'=16] {'row','col'}, dimensions={0} | all-to-all | bytes 262144 | tf_op jit(solution)/shard_map/all_to_all | solution.py:168
  113.8 1.6 shard_map.57
  115.5 1.3 collective-permute-start.6
  116.8 8.0 %collective-permute-done.6.rows_ref = f32[32,1024]{1,0:T(8,128)S(1)} collective-permute-done((f32[32,1024]{1,0:T(8,128)S(1)}, f32[32,1024]{1,0:T(8,128)S(1)}, u32[]{:S(2)}, u32[]{:S(2)}) %collective-permute-start.6) | collective-permute-done | bytes 131104 | tf_op jit(solution)/shard_map/ppermute | solution.py:18
  124.8 1.8 shard_map.58
  126.6 12.3 %all_to_all.38.packed_ref = f32[32,8,128]{2,1,0:T(8,128)S(1)} all-to-all(f32[32,8,128]{2,1,0:T(8,128)S(1)} %shard_map.58), channel_id=1, replica_groups=mesh['days'=8,'row'=2,'col'=16] {'row','col'}, dimensions={0} | all-to-all | bytes 262144 | tf_op jit(solution)/shard_map/all_to_all | solution.py:168
  138.9 1.6 shard_map.59
  140.5 0.0 all-gather.4.cloned.1.call-done
  140.6 1.3 collective-permute-start.8
  141.9 7.1 %collective-permute-done.8.rows_ref = f32[32,1024]{1,0:T(8,128)S(1)} collective-permute-done((f32[32,1024]{1,0:T(8,128)S(1)}, f32[32,1024]{1,0:T(8,128)S(1)}, u32[]{:S(2)}, u32[]{:S(2)}) %collective-permute-start.8) | collective-permute-done | bytes 131104 | tf_op jit(solution)/shard_map/ppermute | solution.py:18
  148.9 2.2 %copy-done.3 = bf16[2,16,64,1024]{3,2,1,0:T(8,128)(2,1)S(1)} copy-done((bf16[2,16,64,1024]{3,2,1,0:T(8,128)(2,1)S(1)}, bf16[2,16,64,1024]{3,2,1,0:T(8,128)(2,1)}, u32[]{:S(2)}) %copy-start.3) | copy-done | bytes 4194328
  151.1 1.8 shard_map.60
  152.9 5.2 %all-to-all-start.5 = ((f32[32,8,128]{2,1,0:T(8,128)}), f32[32,8,128]{2,1,0:T(8,128)S(1)}, u32[]{:S(2)}, u32[]{:S(2)}) async-start(f32[32,8,128]{2,1,0:T(8,128)} %shard_map.60), calls=%async_computation.5 | async-start | bytes 262144 | tf_op jit(solution)/shard_map/all_to_all | solution.py:168
  158.1 0.7 collective-permute-start.9
  158.8 6.8 %all-to-all-done.5.packed_ref = f32[32,8,128]{2,1,0:T(8,128)S(1)} async-done(((f32[32,8,128]{2,1,0:T(8,128)}), f32[32,8,128]{2,1,0:T(8,128)S(1)}, u32[]{:S(2)}, u32[]{:S(2)}) %all-to-all-start.5) | async-done | bytes 131104 | tf_op jit(solution)/shard_map/all_to_all | solution.py:168
  165.6 2.2 %copy-done.4 = bf16[2,16,64,1024]{3,2,1,0:T(8,128)(2,1)S(1)} copy-done((bf16[2,16,64,1024]{3,2,1,0:T(8,128)(2,1)S(1)}, bf16[2,16,64,1024]{3,2,1,0:T(8,128)(2,1)}, u32[]{:S(2)}) %copy-start.4) | copy-done | bytes 4194328
  167.8 0.9 shard_map.61
  168.8 1.1 broadcast_in_dim.8
  169.9 3.7 %all-to-all-start.6 = ((bf16[16,32,1024]{2,1,0:T(8,128)(2,1)}), bf16[16,32,1024]{2,1,0:T(8,128)(2,1)S(1)}, u32[]{:S(2)}, u32[]{:S(2)}) async-start(bf16[16,32,1024]{2,1,0:T(8,128)(2,1)} %broadcast_in_dim.8), calls=%async_computation.6 | async-start | bytes 2097152 | tf_op jit(solution)/shard_map/all_to_all | solution.py:36
  173.6 0.7 collective-permute-start.7
  174.2 15.0 %all-to-all-done.6 = bf16[16,32,1024]{2,1,0:T(8,128)(2,1)S(1)} async-done(((bf16[16,32,1024]{2,1,0:T(8,128)(2,1)}), bf16[16,32,1024]{2,1,0:T(8,128)(2,1)S(1)}, u32[]{:S(2)}, u32[]{:S(2)}) %all-to-all-start.6) | async-done | bytes 1048608 | tf_op jit(solution)/shard_map/all_to_all | solution.py:36
  189.3 3.0 %collective-permute-start.10 = (bf16[16,32,1024]{2,1,0:T(8,128)(2,1)S(1)}, bf16[16,32,1024]{2,1,0:T(8,128)(2,1)}, u32[]{:S(2)}, u32[]{:S(2)}) collective-permute-start(bf16[16,32,1024]{2,1,0:T(8,128)(2,1)S(1)} %all-to-all-done.6), channel_id=1, source_target_pairs={{0,16},{16,0},{1,17},{17,1},{2,18},{18,2},{3,19},{19,3},{4,20},{20... | collective-permute-start | bytes 3145736 | tf_op jit(solution)/shard_map/ppermute | solution.py:22
  192.3 0.1 slice.40
  192.4 2.8 %fusion.6 = (bf16[1,16,64,1024]{3,2,1,0:T(8,128)(2,1)S(1)}, bf16[1,16,64,1024]{3,2,1,0:T(8,128)(2,1)S(1)}) fusion(bf16[2,16,64,1024]{3,2,1,0:T(8,128)(2,1)} %copy-done), kind=kLoop, calls=%fused_computation.31 | loop fusion | bytes 8388608 | tf_op jit(solution)/shard_map/slice | solution.py:227
  195.2 1.5 broadcast_select_fusion.3
  196.7 0.3 pad_maximum_fusion
  197.0 1.4 broadcast_select_fusion.1
  198.3 0.2 pad_maximum_fusion.1
  198.6 2.4 %convolution_convert_fusion = bf16[1024,1024]{1,0:T(8,128)(2,1)S(1)} fusion(bf16[1024,1024]{1,0:T(8,128)(2,1)S(1)} %bitcast.40, bf16[1024,1024]{1,0:T(8,128)(2,1)S(1)} %bitcast.41), kind=kOutput, calls=%fused_computation.4 | convolution fusion | flops 2148532224 | bytes 6291456 | tf_op jit(solution)/shard_map/dot_general | solution.py:172
  200.9 2.6 %fusion = bf16[1024,1024]{1,0:T(8,128)(2,1)S(1)} fusion(bf16[16,64,1024]{2,1,0:T(8,128)(2,1)S(1)} %pad_maximum_fusion, bf16[1024,1024]{1,0:T(8,128)(2,1)S(1)} %bitcast.42, bf16[1024,1024]{1,0:T(8,128)(2,1)S(1)} %convolution_convert_fusion), kind=kOutput, calls=%fused_computation.1 | convolution fusion | flops 2150629376 | bytes 8388608 | tf_op jit(solution)/shard_map/dot_general | solution.py:176
  203.5 1.2 convolution_convert_fusion.1
  204.8 0.4 fusion.2
  205.2 0.7 pad_maximum_fusion.4
  205.9 0.7 pad_maximum_fusion.3
  (32 shorter events, 0.2 us)
Async XLA Ops:
  9.7 7.8 %copy-start.6 = (bf16[2,64,512]{2,1,0:T(8,128)(2,1)S(1)}, bf16[2,64,512]{2,1,0:T(8,128)(2,1)}, u32[]{:S(2)}) copy-start(bf16[2,64,512]{2,1,0:T(8,128)(2,1)} %param.3) | copy-start | bytes 393220
  9.7 7.8 %copy-start.8 = (bf16[64,512]{1,0:T(8,128)(2,1)S(1)}, bf16[64,512]{1,0:T(8,128)(2,1)}, u32[]{:S(2)}) copy-start(bf16[64,512]{1,0:T(8,128)(2,1)} %param.5) | copy-start | bytes 196612
  9.7 8.9 %copy-start.9 = (bf16[2,64,512]{2,1,0:T(8,128)(2,1)S(1)}, bf16[2,64,512]{2,1,0:T(8,128)(2,1)}, u32[]{:S(2)}) copy-start(bf16[2,64,512]{2,1,0:T(8,128)(2,1)} %param.4) | copy-start | bytes 393220
  9.7 35.6 %all-to-all-start = ((bf16[16,2,64,512]{3,2,1,0:T(8,128)(2,1)}), bf16[16,2,64,512]{3,2,1,0:T(8,128)(2,1)S(1)}, u32[]{:S(2)}, u32[]{:S(2)}) async-start(bf16[16,2,64,512]{3,2,1,0:T(8,128)(2,1)} %broadcast_in_dim.6), calls=%async_computation | async-start | bytes 4194304 | tf_op jit(solution)/shard_map/all_to_all | solution.py:36
  17.4 72.7 %all-gather.6.cloned.1.call-start = ((), (), s32[]{:S(2)}) async-start(), calls=%async_computation.8 | async-start | bytes 2228224 | tf_op jit(solution)/shard_map/all_gather | solution.py:193
  17.5 8.3 %collective-permute-start.2 = (bf16[3,64,512]{2,1,0:T(8,128)(2,1)S(1)}, bf16[3,64,512]{2,1,0:T(8,128)(2,1)S(1)}, u32[]{:S(2)}, u32[]{:S(2)}) collective-permute-start(bf16[3,64,512]{2,1,0:T(8,128)(2,1)S(1)} %pad_maximum_fusion.2), channel_id=1, source_target_pairs={{0,16},{16,0},{1,17},{17,1},{2,18},{18,2},{3,19},{19,3},{4,20},{20... | collective-permute-start | bytes 589832 | tf_op jit(solution)/shard_map/ppermute | solution.py:22
  18.5 7.3 %collective-permute-start.1 = (bf16[2,64,512]{2,1,0:T(8,128)(2,1)S(1)}, bf16[2,64,512]{2,1,0:T(8,128)(2,1)S(1)}, u32[]{:S(2)}, u32[]{:S(2)}) collective-permute-start(bf16[2,64,512]{2,1,0:T(8,128)(2,1)S(1)} %copy-done.9), channel_id=1, source_target_pairs={{32,0},{64,32},{96,64},{128,96},{160,128},{192,160},{224,192},{33,... | collective-permute-start | bytes 393224 | tf_op jit(solution)/shard_map/ppermute | solution.py:18
  25.8 0.7 copy-start.10
  26.5 114.1 %all-gather.4.cloned.1.call-start = ((), (), s32[]{:S(2)}) async-start(), calls=%async_computation.7 | async-start | bytes 1114112 | tf_op jit(solution)/shard_map/all_gather | solution.py:214
  45.3 7.5 %collective-permute-start = (bf16[16,2,64,512]{3,2,1,0:T(8,128)(2,1)S(1)}, bf16[16,2,64,512]{3,2,1,0:T(8,128)(2,1)}, u32[]{:S(2)}, u32[]{:S(2)}) collective-permute-start(bf16[16,2,64,512]{3,2,1,0:T(8,128)(2,1)S(1)} %all-to-all-done.own_ref), channel_id=1, source_target_pairs={{0,16},{16,0},{1,17},{17,1},{2,18},{18,2},{3,19},{19,3},{4,20},{20... | collective-permute-start | bytes 6291464 | tf_op jit(solution)/shard_map/ppermute | solution.py:22
  54.5 34.6 %copy-start = (bf16[2,16,64,1024]{3,2,1,0:T(8,128)(2,1)}, bf16[2,16,64,1024]{3,2,1,0:T(8,128)(2,1)S(1)}, u32[]{:S(2)}) copy-start(bf16[2,16,64,1024]{3,2,1,0:T(8,128)(2,1)S(1)} %shard_map.50.factor_ref.refs_0_.refs_1_) | copy-start | bytes 12582916
  69.3 6.8 %collective-permute-start.3 = (f32[32,1024]{1,0:T(8,128)S(1)}, f32[32,1024]{1,0:T(8,128)S(1)}, u32[]{:S(2)}, u32[]{:S(2)}) collective-permute-start(f32[32,1024]{1,0:T(8,128)S(1)} %shard_map.52.base_ref), channel_id=1, source_target_pairs={{32,0},{64,32},{96,64},{128,96},{160,128},{192,160},{224,192},{33,... | collective-permute-start | bytes 393224 | tf_op jit(solution)/shard_map/ppermute | solution.py:18
  90.1 4.8 %collective-permute-start.5 = (bf16[16,2,64,512]{3,2,1,0:T(8,128)(2,1)}, bf16[16,2,64,512]{3,2,1,0:T(8,128)(2,1)}, u32[]{:S(2)}, u32[]{:S(2)}) collective-permute-start(bf16[16,2,64,512]{3,2,1,0:T(8,128)(2,1)} %bitcast.37), channel_id=1, source_target_pairs={{0,16},{16,0},{1,17},{17,1},{2,18},{18,2},{3,19},{19,3},{4,20},{20... | collective-permute-start | bytes 6291464 | tf_op jit(solution)/shard_map/ppermute | solution.py:22
  91.5 9.0 %copy-start.1 = (bf16[2,16,64,1024]{3,2,1,0:T(8,128)(2,1)S(1)}, bf16[2,16,64,1024]{3,2,1,0:T(8,128)(2,1)}, u32[]{:S(2)}) copy-start(bf16[2,16,64,1024]{3,2,1,0:T(8,128)(2,1)} %copy-done) | copy-start | bytes 12582916
  91.5 9.0 %collective-permute-start.4 = (f32[32,1024]{1,0:T(8,128)S(1)}, f32[32,1024]{1,0:T(8,128)S(1)}, u32[]{:S(2)}, u32[]{:S(2)}) collective-permute-start(f32[32,1024]{1,0:T(8,128)S(1)} %shard_map.54.base_ref), channel_id=1, source_target_pairs={{64,0},{128,64},{192,128},{65,1},{129,65},{193,129},{66,2},{130,66... | collective-permute-start | bytes 393224 | tf_op jit(solution)/shard_map/ppermute | solution.py:18
  94.9 1.6 copy-start.5
  98.3 40.6 %copy-start.2 = (bf16[2,16,64,1024]{3,2,1,0:T(8,128)(2,1)}, bf16[2,16,64,1024]{3,2,1,0:T(8,128)(2,1)S(1)}, u32[]{:S(2)}) copy-start(bf16[2,16,64,1024]{3,2,1,0:T(8,128)(2,1)S(1)} %shard_map.55.refs_0_) | copy-start | bytes 12582916
  115.5 9.3 %collective-permute-start.6 = (f32[32,1024]{1,0:T(8,128)S(1)}, f32[32,1024]{1,0:T(8,128)S(1)}, u32[]{:S(2)}, u32[]{:S(2)}) collective-permute-start(f32[32,1024]{1,0:T(8,128)S(1)} %shard_map.57), channel_id=1, source_target_pairs={{64,0},{128,64},{192,128},{65,1},{129,65},{193,129},{66,2},{130,66... | collective-permute-start | bytes 393224 | tf_op jit(solution)/shard_map/ppermute | solution.py:18
  140.6 8.4 %collective-permute-start.8 = (f32[32,1024]{1,0:T(8,128)S(1)}, f32[32,1024]{1,0:T(8,128)S(1)}, u32[]{:S(2)}, u32[]{:S(2)}) collective-permute-start(f32[32,1024]{1,0:T(8,128)S(1)} %shard_map.59), channel_id=1, source_target_pairs={{64,0},{128,64},{192,128},{65,1},{129,65},{193,129},{66,2},{130,66... | collective-permute-start | bytes 393224 | tf_op jit(solution)/shard_map/ppermute | solution.py:18
  148.9 2.2 %copy-start.3 = (bf16[2,16,64,1024]{3,2,1,0:T(8,128)(2,1)S(1)}, bf16[2,16,64,1024]{3,2,1,0:T(8,128)(2,1)}, u32[]{:S(2)}) copy-start(bf16[2,16,64,1024]{3,2,1,0:T(8,128)(2,1)} %copy-done.2) | copy-start | bytes 12582916
  152.9 12.8 %all-to-all-start.5 = ((f32[32,8,128]{2,1,0:T(8,128)}), f32[32,8,128]{2,1,0:T(8,128)S(1)}, u32[]{:S(2)}, u32[]{:S(2)}) async-start(f32[32,8,128]{2,1,0:T(8,128)} %shard_map.60), calls=%async_computation.5 | async-start | bytes 262144 | tf_op jit(solution)/shard_map/all_to_all | solution.py:168
  158.1 10.6 %collective-permute-start.9 = (bf16[32,1024]{1,0:T(8,128)(2,1)S(1)}, bf16[32,1024]{1,0:T(8,128)(2,1)S(1)}, u32[]{:S(2)}, u32[]{:S(2)}) collective-permute-start(bf16[32,1024]{1,0:T(8,128)(2,1)S(1)} %convert_element_type.35), channel_id=1, source_target_pairs={{64,32},{128,96},{192,160},{65,33},{129,97},{193,161},{66,34},{130... | collective-permute-start | bytes 196616 | tf_op jit(solution)/shard_map/ppermute | solution.py:18
  165.6 2.2 %copy-start.4 = (bf16[2,16,64,1024]{3,2,1,0:T(8,128)(2,1)S(1)}, bf16[2,16,64,1024]{3,2,1,0:T(8,128)(2,1)}, u32[]{:S(2)}) copy-start(bf16[2,16,64,1024]{3,2,1,0:T(8,128)(2,1)} %copy-done.2) | copy-start | bytes 12582916
  169.9 19.4 %all-to-all-start.6 = ((bf16[16,32,1024]{2,1,0:T(8,128)(2,1)}), bf16[16,32,1024]{2,1,0:T(8,128)(2,1)S(1)}, u32[]{:S(2)}, u32[]{:S(2)}) async-start(bf16[16,32,1024]{2,1,0:T(8,128)(2,1)} %broadcast_in_dim.8), calls=%async_computation.6 | async-start | bytes 2097152 | tf_op jit(solution)/shard_map/all_to_all | solution.py:36
  173.6 21.6 %collective-permute-start.7 = (bf16[16,64,512]{2,1,0:T(8,128)(2,1)}, bf16[16,64,512]{2,1,0:T(8,128)(2,1)}, u32[]{:S(2)}, u32[]{:S(2)}) collective-permute-start(bf16[16,64,512]{2,1,0:T(8,128)(2,1)} %all-gather.4.cloned.1.call-done), channel_id=1, source_target_pairs={{0,16},{16,0},{1,17},{17,1},{2,18},{18,2},{3,19},{19,3},{4,20},{20... | collective-permute-start | bytes 3145736 | tf_op jit(solution)/shard_map/ppermute | solution.py:22
  189.3 7.7 %collective-permute-start.10 = (bf16[16,32,1024]{2,1,0:T(8,128)(2,1)S(1)}, bf16[16,32,1024]{2,1,0:T(8,128)(2,1)}, u32[]{:S(2)}, u32[]{:S(2)}) collective-permute-start(bf16[16,32,1024]{2,1,0:T(8,128)(2,1)S(1)} %all-to-all-done.6), channel_id=1, source_target_pairs={{0,16},{16,0},{1,17},{17,1},{2,18},{18,2},{3,19},{19,3},{4,20},{20... | collective-permute-start | bytes 3145736 | tf_op jit(solution)/shard_map/ppermute | solution.py:22
  192.4 2.8 %copy-start.7 = (bf16[16,64,512]{2,1,0:T(8,128)(2,1)S(1)}, bf16[16,64,512]{2,1,0:T(8,128)(2,1)}, u32[]{:S(2)}) copy-start(bf16[16,64,512]{2,1,0:T(8,128)(2,1)} %all-gather.4.cloned.1.call-done) | copy-start | bytes 3145732
Sparse Core Ops, SparseCore 0:
  26.6 53.4 all-gather.5
  91.6 45.4 all-gather.3
where the time goes:
time: 214 us; the launch traced here: 213 us
  waiting for transfers between devices  75.1 us (35%)
  blocking collectives  48.3 us (23%)
  starting transfers between devices  33 us (15%)
  Pallas kernels  17.3 us (8%)
  between operations  14.4 us (7%)
  local copies, waits for them, and re-layouts  13.8 us (6%)
  matrix products  6.59 us (3%)
  other arithmetic  4.77 us (2%)
    all_to_all x4, blocking collectives, traded(): return lax.all_to_all(value, ('row', 'col'), 0, 0, tiled=True)  48.3 us
    all_to_all x2, waiting for transfers between devices, spread(): lax.all_to_all(jnp.broadcast_to(value[None], (count,) + value.shape), 'co...  33.8 us
    ppermute x6, waiting for transfers between devices, shifted(): lax.ppermute(value, 'days', [(source, source - steps) for source in sourc...  28.7 us
    pallas_call x10, Pallas kernels, call(): pl.pallas_call(body, out_shape=jax.ShapeDtypeStruct(shape, wide), in_spec...  13.8 us
    all_to_all x2, starting transfers between devices, spread(): lax.all_to_all(jnp.broadcast_to(value[None], (count,) + value.shape), 'co...  11.4 us
    ppermute x5, starting transfers between devices, other_core(): return lax.ppermute(value, 'row', [(0, 1), (1, 0)])  8.96 us
    ppermute x6, starting transfers between devices, shifted(): lax.ppermute(value, 'days', [(source, source - steps) for source in sourc...  7.38 us
    all_to_all x1, waiting for transfers between devices, traded(): return lax.all_to_all(value, ('row', 'col'), 0, 0, tiled=True)  6.83 us
  transfers between devices with their start and end apart: 16, of which 10 were waited for; matrix products, arithmetic and copies ran while one was open for 3% of the time, Pallas kernels for 7%

commit v1 on v0

v1 whole, which is shorter than its diff:
```python
import functools

import jax
import jax.numpy as jnp
from jax import lax
from jax.experimental import pallas as pl
from jax.experimental.pallas import tpu as pltpu
from jax.sharding import PartitionSpec as P

narrow = jnp.bfloat16
wide = jnp.float32
STRIP = 32
PACK = 8
BLOCK = 256
SIDE = 4
VMEM_LIMIT = 20 * 1024 * 1024

vmem = pl.BlockSpec(memory_space=pltpu.VMEM)
hbm = pl.BlockSpec(memory_space=pltpu.HBM)


def params():
    return pltpu.CompilerParams(vmem_limit_bytes=VMEM_LIMIT)


def pinned(value):
    return pltpu.with_memory_space_constraint(value, pltpu.VMEM)


def outside(value):
    return pltpu.with_memory_space_constraint(value, pltpu.HBM)


def hop(value, steps, sources):
    return lax.ppermute(value, "days", [(source, source - steps) for source in sources])


def other_core(value):
    return lax.ppermute(value, "row", [(0, 1), (1, 0)])


def around(value, stride):
    count = lax.axis_size("col")
    return [
        lax.ppermute(
            value,
            "col",
            [
                (chip, chip + ((chip // stride + turn) % SIDE - chip // stride % SIDE) * stride)
                for chip in range(count)
            ],
        )
        for turn in range(1, SIDE)
    ]


def ordered(own, other, axis):
    first = lax.axis_index("row") == 0
    return jnp.concatenate([jnp.where(first, own, other), jnp.where(first, other, own)], axis=axis)


def to_chips(value):
    return lax.all_to_all(value, "col", 0, 0, tiled=True)


def to_devices(value):
    return lax.all_to_all(value, ("row", "col"), 0, 0, tiled=True)


def halves(value):
    high = value.astype(narrow)
    return (high, (value - high.astype(wide)).astype(narrow))


def whole(factor_ref, day):
    _, chips, rows, nodes = factor_ref.shape
    return factor_ref[day].reshape(chips * rows, nodes)


def times(pieces, factor_ref, day):
    return jnp.dot(pieces, whole(factor_ref, day), preferred_element_type=wide)


def times_wide(rows, factor_ref, day):
    split = times(jnp.concatenate(halves(rows), 0), factor_ref, day)
    count = rows.shape[0]
    return split[:count] + split[count:]


def all_days(rows, factor_refs):
    for ref in factor_refs:
        for day in range(ref.shape[0] - 1, -1, -1):
            rows = times_wide(rows, ref, day)
    return rows


def pack(rows, out_ref, place):
    devices = out_ref.shape[0]
    chips = devices // 2
    padded = jnp.concatenate([rows, jnp.zeros((128 - STRIP, rows.shape[1]), wide)], axis=0)
    turned = padded.T
    for core in range(2):
        for chip in range(chips):
            start = (2 * chip + core) * STRIP
            for part in range(STRIP // PACK):
                out_ref[
                    core * chips + chip,
                    place * PACK : (place + 1) * PACK,
                    part * STRIP : (part + 1) * STRIP,
                ] = turned[start + part * PACK : start + (part + 1) * PACK, :STRIP]


def unpack(in_ref, place, rows_ref):
    devices = in_ref.shape[0]
    chips = devices // 2
    for core in range(2):
        for chip in range(chips):
            start = (2 * chip + core) * STRIP
            for part in range(STRIP // PACK):
                rows_ref[part * PACK : (part + 1) * PACK, start : start + STRIP] = in_ref[
                    core * chips + chip,
                    place * PACK : (place + 1) * PACK,
                    part * STRIP : (part + 1) * STRIP,
                ]


def copied(value, chips):
    def body(in_ref, out_ref):
        for chip in range(chips):
            out_ref[chip] = in_ref[...]

    return pl.pallas_call(
        body,
        out_shape=jax.ShapeDtypeStruct((chips,) + value.shape, value.dtype),
        in_specs=[vmem],
        out_specs=vmem,
        compiler_params=params(),
    )(value)


def lined(own, others, stride):
    shape = own.shape

    def body(*refs):
        out_ref = refs[-1]
        place = lax.axis_index("col") // stride % SIDE
        for turn, ref in enumerate(refs[:-1]):
            source = (place + SIDE - turn) % SIDE
            out_ref[pl.ds(source * shape[0], shape[0])] = ref[...]

    return pl.pallas_call(
        body,
        out_shape=jax.ShapeDtypeStruct((SIDE * shape[0],) + shape[1:], own.dtype),
        in_specs=[vmem] * SIDE,
        out_specs=vmem,
        compiler_params=params(),
    )(own, *others)


def staged(own, other):
    days = len(own)
    chips, _, rows, half = own[0][0].shape
    layers = [layer for pair in zip(own, other) for _, layer in pair]

    def body(*refs):
        out_ref, sems = refs[-2:]
        core = lax.axis_index("row")
        copies = []
        for which, layer in enumerate(layers):
            place = core if which % 2 == 0 else 1 - core
            start = pl.multiple_of(place * half, half)
            copies.append(
                pltpu.make_async_copy(
                    refs[which].at[:, layer],
                    out_ref.at[which // 2, :, :, pl.ds(start, half)],
                    sems.at[which],
                )
            )
        for copy in copies:
            copy.start()
        for copy in copies:
            copy.wait()

    return pl.pallas_call(
        body,
        out_shape=pltpu.VMEM((days, chips, rows, 2 * half), narrow),
        in_specs=[hbm] * (2 * days),
        out_specs=vmem,
        scratch_shapes=[pltpu.SemaphoreType.DMA((2 * days,))],
        compiler_params=params(),
    )(*[value for pair in zip(own, other) for value, _ in pair])


def first_out(inverse_ref, sigma_ref, factor_ref, out_ref):
    later = times(sigma_ref[...], factor_ref, 1)
    stacked = jnp.concatenate([inverse_ref[...], *halves(later)], 0)
    split = times(stacked, factor_ref, 0)
    pack(split[:STRIP], out_ref, 0)
    pack(split[STRIP : 2 * STRIP] + split[2 * STRIP :], out_ref, 1)


def first_in(packed_ref, base_ref, factor_ref, out_ref, near_ref, far_ref):
    unpack(packed_ref, 0, near_ref)
    unpack(packed_ref, 1, far_ref)
    later = near_ref[...] + times_wide(far_ref[...], factor_ref, 1)
    out_ref[...] = base_ref[...].astype(wide) + times_wide(later, factor_ref, 0)


def step_out(rows_ref, *refs):
    pack(all_days(rows_ref[...], refs[:-1]), refs[-1], 0)


def step_in(packed_ref, base_ref, *refs):
    out_ref, rows_ref = refs[-2:]
    unpack(packed_ref, 0, rows_ref)
    out_ref[...] = base_ref[...] + all_days(rows_ref[...], refs[:-2])


def last_out(far_ref, next_ref, factor_ref, out_ref):
    part_way = all_days(far_ref[...], [next_ref])
    pack(part_way, out_ref, 0)
    pack(all_days(part_way, [factor_ref]), out_ref, 1)


def last_in(
    packed_ref,
    near_ref,
    state_ref,
    sigma_ref,
    next_ref,
    factor_ref,
    kept_ref,
    out_ref,
    first_ref,
    second_ref,
):
    unpack(packed_ref, 0, first_ref)
    unpack(packed_ref, 1, second_ref)
    stacked = all_days(jnp.concatenate([first_ref[...], second_ref[...]], 0), [next_ref])
    kept = (near_ref[...] + stacked[:STRIP]).astype(narrow)
    final_group = lax.axis_index("days") == lax.axis_size("days") - 1
    kept_ref[...] = jnp.where(final_group, sigma_ref[...], kept)
    before = state_ref[...] + all_days(stacked[STRIP:], [factor_ref])
    out_ref[...] = before.astype(narrow)


def chosen(kept_ref, arrived_ref, out_ref):
    group = lax.axis_index("days")
    keep = (group == 1) | (group == 3) | (group == lax.axis_size("days") - 1)
    separator = jnp.where(keep, kept_ref[...], arrived_ref[...])
    for chip in range(out_ref.shape[0]):
        out_ref[chip] = separator


def inner_days(
    own_ref,
    other_ref,
    factor_ref,
    inverse_own_ref,
    inverse_other_ref,
    inverse_first_ref,
    marginal_ref,
    cross_ref,
    covariance_ref,
    cross_last_ref,
    marginal_last_ref,
    cross_first_ref,
):
    core = lax.axis_index("row")
    chip = lax.axis_index("col")
    _, chips, rows, nodes = factor_ref.shape
    half = nodes // 2
    for place in range(chips):
        for ref, which in ((own_ref, core), (other_ref, 1 - core)):
            start = pl.multiple_of(place * rows + which * STRIP, STRIP)
            covariance_ref[pl.ds(start, STRIP)] = ref[place]
    for start in range(0, nodes, BLOCK):
        cross_last_ref[start : start + BLOCK] = times(
            covariance_ref[start : start + BLOCK], factor_ref, 1
        ).astype(narrow)
    for block in range(nodes // BLOCK):
        start = block * BLOCK
        factor_cols = factor_ref[1, :, :, start : start + BLOCK].reshape(nodes, BLOCK)
        summed = lax.dot_general(
            factor_cols,
            cross_last_ref[...],
            (((0,), (0,)), ((), ())),
            preferred_element_type=wide,
        )
        layers = slice(start // rows, (start + BLOCK) // rows)
        own = inverse_own_ref[layers].reshape(BLOCK, half)
        other = inverse_other_ref[layers].reshape(BLOCK, half)
        left = jnp.where(core == 0, own, other).astype(wide) + summed[:, :half]
        right = jnp.where(core == 0, other, own).astype(wide) + summed[:, half:]
        marginal_last_ref[start : start + BLOCK, :half] = left.astype(narrow)
        marginal_last_ref[start : start + BLOCK, half:] = right.astype(narrow)
    columns = pl.ds(pl.multiple_of(core * half, half), half)
    first_half = factor_ref[0, :, :, columns].reshape(nodes, half)
    for start in range(0, nodes, BLOCK):
        cross_first_ref[start : start + BLOCK] = jnp.dot(
            marginal_last_ref[start : start + BLOCK], first_half, preferred_element_type=wide
        ).astype(narrow)
    near = pl.ds(pl.multiple_of((chip // 2) * 2 * rows, 2 * rows), 2 * rows)
    summed = lax.dot_general(
        factor_ref[0, :, :, near].reshape(nodes, 2 * rows),
        cross_first_ref[...],
        (((0,), (0,)), ((), ())),
        preferred_element_type=wide,
    )
    summed = jnp.where(chip % 2 == 0, summed[:rows], summed[rows:])
    mine = pl.ds(pl.multiple_of(chip * rows, rows), rows)
    marginal_ref[0] = (inverse_first_ref[...].astype(wide) + summed).astype(narrow)
    marginal_ref[1] = marginal_last_ref[mine, columns]
    cross_ref[0] = cross_first_ref[mine]
    cross_ref[1] = cross_last_ref[mine, columns]


def call(body, outs, scratch, operands, factors):
    single = not isinstance(outs, list)
    return pl.pallas_call(
        body,
        out_shape=outs if single else tuple(outs),
        in_specs=[vmem] * (len(operands) + len(factors)),
        out_specs=vmem if single else tuple([vmem] * len(outs)),
        scratch_shapes=scratch,
        compiler_params=params(),
    )(*operands, *[pinned(factor) for factor in factors])


def shards(inverse_blocks, factor_blocks, sigma_end):
    chips = lax.axis_size("col")
    days, rows, half = factor_blocks.shape
    nodes = chips * rows
    devices = 2 * chips
    core = lax.axis_index("row")
    final_group = lax.axis_index("days") == lax.axis_size("days") - 1

    fixed = jnp.stack([inverse_blocks[0], inverse_blocks[1], sigma_end])
    fixed = ordered(fixed, other_core(fixed), 2)
    strips = lax.dynamic_slice_in_dim(fixed, core * STRIP, STRIP, 1)
    base, last_strip, sigma_strip = (strips[0], strips[1], strips[2])
    started = jnp.where(final_group, sigma_strip, jnp.zeros_like(sigma_strip))

    mine = to_chips(copied(factor_blocks, chips))
    inverse_last = inverse_blocks[1:]
    inverse_line = lined(inverse_last, around(inverse_last, 1), 1)
    (mine, mine_first, mine_last, inverse_line, base, last_strip, sigma_strip, started) = (
        lax.optimization_barrier(
            (
                mine,
                mine[:, :1],
                mine[:, 1:],
                inverse_line,
                base,
                last_strip,
                sigma_strip,
                started,
            )
        )
    )
    next_last = hop(mine_last, 1, (2, 4))
    theirs = other_core(mine)
    own = staged([(mine, 0), (mine, 1)], [(theirs, 0), (theirs, 1)])

    strip = (STRIP, nodes)
    state_shape = jax.ShapeDtypeStruct(strip, wide)
    rows_scratch = pltpu.VMEM(strip, wide)

    def packed_shape(count):
        return jax.ShapeDtypeStruct((devices, count * PACK, 128), wide)

    packed = call(first_out, packed_shape(2), [], [last_strip, started], [own])
    first_state = call(
        first_in, state_shape, [rows_scratch] * 2, [to_devices(packed), base], [own]
    )

    def step(base, arrived, factors):
        packed = call(step_out, packed_shape(1), [], [arrived], factors)
        return call(
            step_in, state_shape, [rows_scratch], [to_devices(packed), base], factors
        )

    near, mine_first, next_last = lax.optimization_barrier(
        (hop(first_state, 1, (2, 4, 7)), mine_first, next_last)
    )
    next_first = hop(mine_first, 1, (2, 4))
    state = step(first_state, near, [own])
    state = step(state, hop(state, 1, (6,)), [own])

    pair_state, next_first, beside = lax.optimization_barrier(
        (state, next_first, around(inverse_line, SIDE))
    )
    far = hop(pair_state, 2, (5,))
    inverse_mine = lined(inverse_line, beside, SIDE)
    following = staged(
        [(outside(next_first), 0), (outside(next_last), 0)],
        [(outside(other_core(next_first)), 0), (outside(other_core(next_last)), 0)],
    )
    factors = [following, own]
    state = step(pair_state, far, factors)
    far, inverse_theirs = lax.optimization_barrier(
        (hop(state, 2, (3, 5)), other_core(inverse_mine))
    )
    packed = call(last_out, packed_shape(2), [], [far], factors)
    strip_narrow = jax.ShapeDtypeStruct(strip, narrow)
    kept, before = call(
        last_in,
        [strip_narrow, strip_narrow],
        [rows_scratch] * 2,
        [to_devices(packed), near, pair_state, sigma_strip],
        factors,
    )
    copies = call(
        chosen,
        jax.ShapeDtypeStruct((chips,) + strip, narrow),
        [],
        [kept, hop(before, 1, (1, 3, 5, 6, 7))],
        [],
    )
    separator = to_chips(copies)
    block = jax.ShapeDtypeStruct((days, rows, half), narrow)
    square = pltpu.VMEM((nodes, nodes), narrow)
    return pl.pallas_call(
        inner_days,
        out_shape=(block, block),
        in_specs=[vmem] * 6,
        out_specs=(vmem, vmem),
        scratch_shapes=[square] * 3 + [pltpu.VMEM((nodes, half), narrow)],
        compiler_params=params(),
    )(
        separator,
        other_core(separator),
        pinned(own),
        inverse_mine,
        inverse_theirs,
        inverse_blocks[0],
    )


def solution(mesh):
    placed = (P("days", "col", "row"), P("days", "col", "row"), P("col", "row"))
    return jax.shard_map(
        shards,
        mesh=mesh,
        in_specs=placed,
        out_specs=(P("days", "col", "row"), P("days", "col", "row")),
        check_vma=False,
    )
```

time: 214 us -> 197 us (0.921)
  between operations: 14.4 us -> 0.99 us
  waiting for transfers between devices: 75.1 us -> 62.2 us
  blocking collectives: 48.3 us -> 56.8 us
  starting transfers between devices: 33 us -> 41.3 us
  Pallas kernels: 17.3 us -> 24.4 us
  matrix products: 6.59 us -> 0 us
  other arithmetic: 4.77 us -> 0.1 us
  local copies, waits for them, and re-layouts: 13.8 us -> 10.9 us
    all_to_all x3, waiting for transfers between devices: 40.6 us -> 10.1 us  [the longest x2 9.78 us: to_devices(): return lax.all_to_all(value, ('row', 'col'), 0, 0, tiled=True)]
    ppermute x6 -> x13, waiting for transfers between devices: 28.7 us -> 45.1 us  [the longest x7 24.1 us: hop(): lax.ppermute(value, 'days', [(source, source - steps) for source in sourc...]
    ppermute x6 -> x13, starting transfers between devices: 7.38 us -> 16.8 us  [the longest x6 10.4 us: around(): lax.ppermute(value, 'col', [(chip, chip + ((chip // stride + turn) % SIDE...]
    all_to_all x4, blocking collectives: 48.3 us -> 56.8 us  [the longest x3 37.7 us: to_devices(): return lax.all_to_all(value, ('row', 'col'), 0, 0, tiled=True)]
    pallas_call x12 -> x17, Pallas kernels: 17.3 us -> 24.4 us  [the longest x11 14.6 us: call(): pl.pallas_call(body, out_shape=outs if single else tuple(outs), in_specs=...]
    dot_general x4 -> x0, matrix products: 6.59 us -> none  [the longest x2 3.6 us: product(): return jnp.dot(left, right, preferred_element_type=wide)]
    broadcast_in_dim x2 -> x0, local copies, waits for them, and re-layouts: 3.64 us -> none  [spread(): jnp.broadcast_to(value[None], (count,) + value.shape)]
    unnamed x22, local copies, waits for them, and re-layouts: 6.65 us -> 9.7 us
  transfers between devices with their start and end apart: 16 -> 22, of which waited for: 10 -> 8; matrix products, arithmetic and copies ran while one was open for 3% -> 0% of each run, Pallas kernels for 7% -> 7%
where the time goes in v1:
time: 197 us
  waiting for transfers between devices  62.2 us (32%)
  blocking collectives  56.8 us (29%)
  starting transfers between devices  41.3 us (21%)
  Pallas kernels  24.4 us (12%)
  local copies, waits for them, and re-layouts  10.9 us (6%)
    all_to_all x3, blocking collectives, to_devices(): return lax.all_to_all(value, ('row', 'col'), 0, 0, tiled=True)  37.7 us
    ppermute x7, waiting for transfers between devices, hop(): lax.ppermute(value, 'days', [(source, source - steps) for source in sourc...  24.1 us
    ppermute x6, waiting for transfers between devices, around(): lax.ppermute(value, 'col', [(chip, chip + ((chip // stride + turn) % SIDE...  21 us
    all_to_all x1, blocking collectives, to_chips(): return lax.all_to_all(value, 'col', 0, 0, tiled=True)  19.1 us
    pallas_call x11, Pallas kernels, call(): pl.pallas_call(body, out_shape=outs if single else tuple(outs), in_specs=...  14.6 us
    ppermute x6, starting transfers between devices, around(): lax.ppermute(value, 'col', [(chip, chip + ((chip // stride + turn) % SIDE...  10.4 us
    all_to_all x2, waiting for transfers between devices, to_devices(): return lax.all_to_all(value, ('row', 'col'), 0, 0, tiled=True)  9.78 us
    unnamed x22, local copies, waits for them, and re-layouts  9.7 us
  transfers between devices with their start and end apart: 22, of which 8 were waited for; matrix products, arithmetic and copies ran while one was open for 0% of the time, Pallas kernels for 7%

profile of v1, /device:TPU:1, one launch (start us, length us, event | category | flops | bytes accessed | tf_op | source)
XLA Modules:
  0.0 196.6 jit_solution(12753264300962812026)
XLA Ops:
  0.6 0.9 copy-done.5
  1.5 0.1 shard_map.50
  1.7 1.3 copy-done.4
  3.0 7.7 %all-to-all-start = ((bf16[16,2,64,512]{3,2,1,0:T(8,128)(2,1)}), bf16[16,2,64,512]{3,2,1,0:T(8,128)(2,1)S(1)}, u32[]{:S(2)}, u32[]{:S(2)}) async-start(bf16[16,2,64,512]{3,2,1,0:T(8,128)(2,1)} %copy-done.4), calls=%async_computation | async-start | bytes 4194304 | tf_op jit(solution)/shard_map/all_to_all | solution.py:63
  10.8 1.0 collective-permute-start.3
  11.9 1.7 collective-permute-start
  13.6 2.4 %collective-permute-start.1 = (bf16[1,64,512]{2,1,0:T(8,128)(2,1)S(1)}, bf16[1,64,512]{2,1,0:T(8,128)(2,1)S(1)}, u32[]{:S(2)}, u32[]{:S(2)}) collective-permute-start(bf16[1,64,512]{2,1,0:T(8,128)(2,1)S(1)} %get-tuple-element.50.refs_0_), channel_id=1, source_target_pairs={{0,2},{1,3},{2,0},{3,1},{4,6},{5,7},{6,4},{7,5},{8,10},{9,11},{10,... | collective-permute-start | bytes 196616 | tf_op jit(solution)/shard_map/ppermute | solution.py:45
  16.0 1.2 collective-permute-start.2
  17.2 21.0 %collective-permute-done.refs_1_ = bf16[1,64,512]{2,1,0:T(8,128)(2,1)S(1)} collective-permute-done((bf16[1,64,512]{2,1,0:T(8,128)(2,1)S(1)}, bf16[1,64,512]{2,1,0:T(8,128)(2,1)S(1)}, u32[]{:S(2)}, u32[]{:S(2)}) %collective-permute-start) | collective-permute-done | bytes 65568 | tf_op jit(solution)/shard_map/ppermute | solution.py:45
  38.1 0.0 collective-permute-done.1.refs_2_
  38.3 0.3 all-to-all-done.refs_0_.refs_2_
  38.6 1.2 fusion.1
  39.8 3.5 %collective-permute-start.4 = (bf16[16,2,64,512]{3,2,1,0:T(8,128)(2,1)S(1)}, bf16[16,2,64,512]{3,2,1,0:T(8,128)(2,1)S(1)}, u32[]{:S(2)}, u32[]{:S(2)}) collective-permute-start(bf16[16,2,64,512]{3,2,1,0:T(8,128)(2,1)S(1)} %all-to-all-done.refs_0_.refs_2_), channel_id=1, source_target_pairs={{0,16},{16,0},{1,17},{17,1},{2,18},{18,2},{3,19},{19,3},{4,20},{20... | collective-permute-start | bytes 6291464 | tf_op jit(solution)/shard_map/ppermute | solution.py:39
  43.3 0.7 collective-permute-start.6
  44.0 3.1 %collective-permute-done.4.refs_1_.refs_3_ = bf16[16,2,64,512]{3,2,1,0:T(8,128)(2,1)S(1)} collective-permute-done((bf16[16,2,64,512]{3,2,1,0:T(8,128)(2,1)S(1)}, bf16[16,2,64,512]{3,2,1,0:T(8,128)(2,1)S(1)}, u32[]{:S(2)}, u32[]{:S(2)}) %collective-permute-start.4) | collective-permute-done | bytes 2097184 | tf_op jit(solution)/shard_map/ppermute | solution.py:39
  47.1 0.7 shard_map.52.factor_ref.refs_0_.refs_1_
  47.8 1.3 shard_map.53
  49.0 14.1 %all_to_all.35.packed_ref = f32[32,16,128]{2,1,0:T(8,128)S(1)} all-to-all(f32[32,16,128]{2,1,0:T(8,128)S(1)} %shard_map.53), channel_id=1, replica_groups=mesh['days'=8,'row'=2,'col'=16] {'row','col'}, dimensions={0} | all-to-all | bytes 524288 | tf_op jit(solution)/shard_map/all_to_all | solution.py:67
  63.1 0.9 shard_map.54.base_ref
  64.0 0.7 collective-permute-start.5
  64.7 0.0 collective-permute-done.6.refs_2_
  64.7 0.0 collective-permute-done.5.rows_ref.near_ref
  64.7 1.0 copy-done.7
  65.7 1.7 collective-permute-start.8
  67.4 1.8 shard_map.55
  69.1 4.3 %all-to-all-start.2 = ((f32[32,8,128]{2,1,0:T(8,128)}), f32[32,8,128]{2,1,0:T(8,128)S(1)}, u32[]{:S(2)}, u32[]{:S(2)}) async-start(f32[32,8,128]{2,1,0:T(8,128)} %shard_map.55), calls=%async_computation.2 | async-start | bytes 262144 | tf_op jit(solution)/shard_map/all_to_all | solution.py:67
  73.4 1.5 collective-permute-start.9
  74.9 2.4 %collective-permute-start.10 = (bf16[4,64,512]{2,1,0:T(8,128)(2,1)S(1)}, bf16[4,64,512]{2,1,0:T(8,128)(2,1)S(1)}, u32[]{:S(2)}, u32[]{:S(2)}) collective-permute-start(bf16[4,64,512]{2,1,0:T(8,128)(2,1)S(1)} %shard_map.51.refs_0_), channel_id=1, source_target_pairs={{0,8},{1,9},{2,10},{3,11},{4,12},{5,13},{6,14},{7,15},{8,0},{9,1},... | collective-permute-start | bytes 786440 | tf_op jit(solution)/shard_map/ppermute | solution.py:45
  77.3 1.2 collective-permute-start.11
  78.5 2.8 %all-to-all-done.2.packed_ref = f32[32,8,128]{2,1,0:T(8,128)S(1)} async-done(((f32[32,8,128]{2,1,0:T(8,128)}), f32[32,8,128]{2,1,0:T(8,128)S(1)}, u32[]{:S(2)}, u32[]{:S(2)}) %all-to-all-start.2) | async-done | bytes 131104 | tf_op jit(solution)/shard_map/all_to_all | solution.py:67
  81.2 2.2 %copy-done.1 = bf16[2,16,64,1024]{3,2,1,0:T(8,128)(2,1)S(1)} copy-done((bf16[2,16,64,1024]{3,2,1,0:T(8,128)(2,1)S(1)}, bf16[2,16,64,1024]{3,2,1,0:T(8,128)(2,1)}, u32[]{:S(2)}) %copy-start.1) | copy-done | bytes 4194328
  83.4 0.9 shard_map.56.base_ref
  84.3 0.0 copy-start.8
  84.3 0.8 collective-permute-start.7
  85.1 1.8 shard_map.57
  86.9 4.3 %all-to-all-start.3 = ((f32[32,8,128]{2,1,0:T(8,128)}), f32[32,8,128]{2,1,0:T(8,128)S(1)}, u32[]{:S(2)}, u32[]{:S(2)}) async-start(f32[32,8,128]{2,1,0:T(8,128)} %shard_map.57), calls=%async_computation.3 | async-start | bytes 262144 | tf_op jit(solution)/shard_map/all_to_all | solution.py:67
  91.2 0.5 collective-permute-start.14
  91.7 7.0 %all-to-all-done.3.packed_ref = f32[32,8,128]{2,1,0:T(8,128)S(1)} async-done(((f32[32,8,128]{2,1,0:T(8,128)}), f32[32,8,128]{2,1,0:T(8,128)S(1)}, u32[]{:S(2)}, u32[]{:S(2)}) %all-to-all-start.3) | async-done | bytes 131104 | tf_op jit(solution)/shard_map/all_to_all | solution.py:67
  98.7 2.2 %copy-done.2 = bf16[2,16,64,1024]{3,2,1,0:T(8,128)(2,1)S(1)} copy-done((bf16[2,16,64,1024]{3,2,1,0:T(8,128)(2,1)S(1)}, bf16[2,16,64,1024]{3,2,1,0:T(8,128)(2,1)}, u32[]{:S(2)}) %copy-start.2) | copy-done | bytes 4194328
  100.9 0.9 shard_map.58.base_ref.state_ref
  101.8 0.0 collective-permute-done.9.refs_1_
  101.8 0.0 collective-permute-done.10.refs_2_
  101.9 0.7 collective-permute-start.13
  102.6 0.1 shard_map.62.inverse_own_ref
  102.7 0.1 collective-permute-start.16
  102.8 0.7 collective-permute-start.12
  103.4 1.6 collective-permute-done.13.refs_1_
  105.1 1.0 copy-done.9
  106.1 2.4 %shard_map.59.refs_0_.next_ref = bf16[2,16,64,1024]{3,2,1,0:T(8,128)(2,1)S(1)} custom-call(bf16[16,1,64,512]{3,2,1,0:T(8,128)(2,1)} %collective-permute-done.8.refs_0_, bf16[16,1,64,512]{3,2,1,0:T(8,128)(2,1)} %copy-done.9, bf16[16,1,64,512]{3,2,1,0:T(8,128)(2,1)} %copy-done.7, bf16[16,1,64,512]{3,2,1,0:T(8,128)(2,1)} %collective-permute-done.14.refs_3_), custom_call_target="tpu_custom_call" | custom-call | tf_op jit(solution)/shard_map/pallas_call | solution.py:184
  108.4 1.1 copy-done.3
  109.5 1.8 shard_map.60
  111.4 11.0 %all_to_all.36.packed_ref = f32[32,8,128]{2,1,0:T(8,128)S(1)} all-to-all(f32[32,8,128]{2,1,0:T(8,128)S(1)} %shard_map.60), channel_id=1, replica_groups=mesh['days'=8,'row'=2,'col'=16] {'row','col'}, dimensions={0} | all-to-all | bytes 262144 | tf_op jit(solution)/shard_map/all_to_all | solution.py:67
  122.4 1.6 shard_map.61
  124.0 0.7 collective-permute-start.15
  124.7 1.9 shard_map.63
  126.6 12.6 %all_to_all.37.packed_ref = f32[32,16,128]{2,1,0:T(8,128)S(1)} all-to-all(f32[32,16,128]{2,1,0:T(8,128)S(1)} %shard_map.63), channel_id=1, replica_groups=mesh['days'=8,'row'=2,'col'=16] {'row','col'}, dimensions={0} | all-to-all | bytes 524288 | tf_op jit(solution)/shard_map/all_to_all | solution.py:67
  139.2 1.7 shard_map.64
  140.9 1.3 collective-permute-start.17
  142.2 24.1 %collective-permute-done.17.arrived_ref = bf16[32,1024]{1,0:T(8,128)(2,1)S(1)} collective-permute-done((bf16[32,1024]{1,0:T(8,128)(2,1)S(1)}, bf16[32,1024]{1,0:T(8,128)(2,1)S(1)}, u32[]{:S(2)}, u32[]{:S(2)}) %collective-permute-start.17) | collective-permute-done | bytes 65568 | tf_op jit(solution)/shard_map/ppermute | solution.py:35
  166.3 0.1 shard_map.65
  166.4 19.1 %all_to_all.38.own_ref = bf16[16,32,1024]{2,1,0:T(8,128)(2,1)S(1)} all-to-all(bf16[16,32,1024]{2,1,0:T(8,128)(2,1)S(1)} %shard_map.65), channel_id=1, replica_groups=mesh['days'=8,'row'=2,'col'=16] {'col'}, dimensions={0} | all-to-all | bytes 2097152 | tf_op jit(solution)/shard_map/all_to_all | solution.py:63
  185.5 2.4 %collective-permute-start.18 = (bf16[16,32,1024]{2,1,0:T(8,128)(2,1)S(1)}, bf16[16,32,1024]{2,1,0:T(8,128)(2,1)S(1)}, u32[]{:S(2)}, u32[]{:S(2)}) collective-permute-start(bf16[16,32,1024]{2,1,0:T(8,128)(2,1)S(1)} %all_to_all.38.own_ref), channel_id=1, source_target_pairs={{0,16},{16,0},{1,17},{17,1},{2,18},{18,2},{3,19},{19,3},{4,20},{20... | collective-permute-start | bytes 3145736 | tf_op jit(solution)/shard_map/ppermute | solution.py:39
  187.9 2.3 %collective-permute-done.18.other_ref = bf16[16,32,1024]{2,1,0:T(8,128)(2,1)S(1)} collective-permute-done((bf16[16,32,1024]{2,1,0:T(8,128)(2,1)S(1)}, bf16[16,32,1024]{2,1,0:T(8,128)(2,1)S(1)}, u32[]{:S(2)}, u32[]{:S(2)}) %collective-permute-start.18) | collective-permute-done | bytes 1048608 | tf_op jit(solution)/shard_map/ppermute | solution.py:39
  190.1 6.5 %shard_map.66 = (bf16[2,64,512]{2,1,0:T(8,128)(2,1)}, bf16[2,64,512]{2,1,0:T(8,128)(2,1)}) custom-call(bf16[16,32,1024]{2,1,0:T(8,128)(2,1)S(1)} %all_to_all.38.own_ref, bf16[16,32,1024]{2,1,0:T(8,128)(2,1)S(1)} %collective-permute-done.18.other_ref, bf16[2,16,64,1024]{3,2,1,0:T(8,128)(2,1)S(1)} %copy-done.3, ...), custom_call_target="tpu_custom_call" | custom-call | tf_op jit(solution)/shard_map/pallas_call | solution.py:423
  (30 shorter events, 0.2 us)
Async XLA Ops:
  0.6 0.9 copy-start.5
  1.7 1.4 copy-start.4
  3.0 7.7 %copy-start.6 = (bf16[2,64,512]{2,1,0:T(8,128)(2,1)S(1)}, bf16[2,64,512]{2,1,0:T(8,128)(2,1)}, u32[]{:S(2)}) copy-start(bf16[2,64,512]{2,1,0:T(8,128)(2,1)} %param.3) | copy-start | bytes 393220
  3.0 7.7 %copy-start.10 = (bf16[64,512]{1,0:T(8,128)(2,1)S(1)}, bf16[64,512]{1,0:T(8,128)(2,1)}, u32[]{:S(2)}) copy-start(bf16[64,512]{1,0:T(8,128)(2,1)} %param.5) | copy-start | bytes 196612
  3.0 35.6 %all-to-all-start = ((bf16[16,2,64,512]{3,2,1,0:T(8,128)(2,1)}), bf16[16,2,64,512]{3,2,1,0:T(8,128)(2,1)S(1)}, u32[]{:S(2)}, u32[]{:S(2)}) async-start(bf16[16,2,64,512]{3,2,1,0:T(8,128)(2,1)} %copy-done.4), calls=%async_computation | async-start | bytes 4194304 | tf_op jit(solution)/shard_map/all_to_all | solution.py:63
  10.8 27.4 %collective-permute-start.3 = (bf16[3,64,512]{2,1,0:T(8,128)(2,1)S(1)}, bf16[3,64,512]{2,1,0:T(8,128)(2,1)S(1)}, u32[]{:S(2)}, u32[]{:S(2)}) collective-permute-start(bf16[3,64,512]{2,1,0:T(8,128)(2,1)S(1)} %pad_maximum_fusion), channel_id=1, source_target_pairs={{0,16},{16,0},{1,17},{17,1},{2,18},{18,2},{3,19},{19,3},{4,20},{20... | collective-permute-start | bytes 589832 | tf_op jit(solution)/shard_map/ppermute | solution.py:39
  11.9 26.3 %collective-permute-start = (bf16[1,64,512]{2,1,0:T(8,128)(2,1)S(1)}, bf16[1,64,512]{2,1,0:T(8,128)(2,1)S(1)}, u32[]{:S(2)}, u32[]{:S(2)}) collective-permute-start(bf16[1,64,512]{2,1,0:T(8,128)(2,1)S(1)} %get-tuple-element.50.refs_0_), channel_id=1, source_target_pairs={{0,1},{1,2},{2,3},{3,0},{4,5},{5,6},{6,7},{7,4},{8,9},{9,10},{10,1... | collective-permute-start | bytes 196616 | tf_op jit(solution)/shard_map/ppermute | solution.py:45
  13.6 24.5 %collective-permute-start.1 = (bf16[1,64,512]{2,1,0:T(8,128)(2,1)S(1)}, bf16[1,64,512]{2,1,0:T(8,128)(2,1)S(1)}, u32[]{:S(2)}, u32[]{:S(2)}) collective-permute-start(bf16[1,64,512]{2,1,0:T(8,128)(2,1)S(1)} %get-tuple-element.50.refs_0_), channel_id=1, source_target_pairs={{0,2},{1,3},{2,0},{3,1},{4,6},{5,7},{6,4},{7,5},{8,10},{9,11},{10,... | collective-permute-start | bytes 196616 | tf_op jit(solution)/shard_map/ppermute | solution.py:45
  16.0 22.1 %collective-permute-start.2 = (bf16[1,64,512]{2,1,0:T(8,128)(2,1)S(1)}, bf16[1,64,512]{2,1,0:T(8,128)(2,1)S(1)}, u32[]{:S(2)}, u32[]{:S(2)}) collective-permute-start(bf16[1,64,512]{2,1,0:T(8,128)(2,1)S(1)} %get-tuple-element.50.refs_0_), channel_id=1, source_target_pairs={{0,3},{1,0},{2,1},{3,2},{4,7},{5,4},{6,5},{7,6},{8,11},{9,8},{10,9... | collective-permute-start | bytes 196616 | tf_op jit(solution)/shard_map/ppermute | solution.py:45
  39.8 7.2 %collective-permute-start.4 = (bf16[16,2,64,512]{3,2,1,0:T(8,128)(2,1)S(1)}, bf16[16,2,64,512]{3,2,1,0:T(8,128)(2,1)S(1)}, u32[]{:S(2)}, u32[]{:S(2)}) collective-permute-start(bf16[16,2,64,512]{3,2,1,0:T(8,128)(2,1)S(1)} %all-to-all-done.refs_0_.refs_2_), channel_id=1, source_target_pairs={{0,16},{16,0},{1,17},{17,1},{2,18},{18,2},{3,19},{19,3},{4,20},{20... | collective-permute-start | bytes 6291464 | tf_op jit(solution)/shard_map/ppermute | solution.py:39
  43.3 21.4 %collective-permute-start.6 = (bf16[16,1,64,512]{3,2,1,0:T(8,128)(2,1)S(1)}, bf16[16,1,64,512]{3,2,1,0:T(8,128)(2,1)S(1)}, u32[]{:S(2)}, u32[]{:S(2)}) collective-permute-start(bf16[16,1,64,512]{3,2,1,0:T(8,128)(2,1)S(1)} %get-tuple-element.27), channel_id=1, source_target_pairs={{64,32},{128,96},{65,33},{129,97},{66,34},{130,98},{67,35},{131,99... | collective-permute-start | bytes 3145736 | tf_op jit(solution)/shard_map/ppermute | solution.py:35
  47.8 19.6 %copy-start = (bf16[2,16,64,1024]{3,2,1,0:T(8,128)(2,1)}, bf16[2,16,64,1024]{3,2,1,0:T(8,128)(2,1)S(1)}, u32[]{:S(2)}) copy-start(bf16[2,16,64,1024]{3,2,1,0:T(8,128)(2,1)S(1)} %shard_map.52.factor_ref.refs_0_.refs_1_) | copy-start | bytes 12582916
  64.0 0.7 collective-permute-start.5
  64.7 1.0 copy-start.7
  65.7 36.2 %collective-permute-start.8 = (bf16[16,1,64,512]{3,2,1,0:T(8,128)(2,1)}, bf16[16,1,64,512]{3,2,1,0:T(8,128)(2,1)}, u32[]{:S(2)}, u32[]{:S(2)}) collective-permute-start(bf16[16,1,64,512]{3,2,1,0:T(8,128)(2,1)} %get-tuple-element.29), channel_id=1, source_target_pairs={{64,32},{128,96},{65,33},{129,97},{66,34},{130,98},{67,35},{131,99... | collective-permute-start | bytes 3145736 | tf_op jit(solution)/shard_map/ppermute | solution.py:35
  69.1 12.1 %all-to-all-start.2 = ((f32[32,8,128]{2,1,0:T(8,128)}), f32[32,8,128]{2,1,0:T(8,128)S(1)}, u32[]{:S(2)}, u32[]{:S(2)}) async-start(f32[32,8,128]{2,1,0:T(8,128)} %shard_map.55), calls=%async_computation.2 | async-start | bytes 262144 | tf_op jit(solution)/shard_map/all_to_all | solution.py:67
  73.4 28.4 %collective-permute-start.9 = (bf16[4,64,512]{2,1,0:T(8,128)(2,1)S(1)}, bf16[4,64,512]{2,1,0:T(8,128)(2,1)S(1)}, u32[]{:S(2)}, u32[]{:S(2)}) collective-permute-start(bf16[4,64,512]{2,1,0:T(8,128)(2,1)S(1)} %shard_map.51.refs_0_), channel_id=1, source_target_pairs={{0,4},{1,5},{2,6},{3,7},{4,8},{5,9},{6,10},{7,11},{8,12},{9,13},{1... | collective-permute-start | bytes 786440 | tf_op jit(solution)/shard_map/ppermute | solution.py:45
  74.9 27.0 %collective-permute-start.10 = (bf16[4,64,512]{2,1,0:T(8,128)(2,1)S(1)}, bf16[4,64,512]{2,1,0:T(8,128)(2,1)S(1)}, u32[]{:S(2)}, u32[]{:S(2)}) collective-permute-start(bf16[4,64,512]{2,1,0:T(8,128)(2,1)S(1)} %shard_map.51.refs_0_), channel_id=1, source_target_pairs={{0,8},{1,9},{2,10},{3,11},{4,12},{5,13},{6,14},{7,15},{8,0},{9,1},... | collective-permute-start | bytes 786440 | tf_op jit(solution)/shard_map/ppermute | solution.py:45
  77.3 24.6 %collective-permute-start.11 = (bf16[4,64,512]{2,1,0:T(8,128)(2,1)S(1)}, bf16[4,64,512]{2,1,0:T(8,128)(2,1)S(1)}, u32[]{:S(2)}, u32[]{:S(2)}) collective-permute-start(bf16[4,64,512]{2,1,0:T(8,128)(2,1)S(1)} %shard_map.51.refs_0_), channel_id=1, source_target_pairs={{0,12},{1,13},{2,14},{3,15},{4,0},{5,1},{6,2},{7,3},{8,4},{9,5},{1... | collective-permute-start | bytes 786440 | tf_op jit(solution)/shard_map/ppermute | solution.py:45
  81.2 2.2 %copy-start.1 = (bf16[2,16,64,1024]{3,2,1,0:T(8,128)(2,1)S(1)}, bf16[2,16,64,1024]{3,2,1,0:T(8,128)(2,1)}, u32[]{:S(2)}) copy-start(bf16[2,16,64,1024]{3,2,1,0:T(8,128)(2,1)} %copy-done) | copy-start | bytes 12582916
  84.3 6.9 %copy-start.8 = (bf16[16,1,64,512]{3,2,1,0:T(8,128)(2,1)S(1)}, bf16[16,1,64,512]{3,2,1,0:T(8,128)(2,1)}, u32[]{:S(2)}) copy-start(bf16[16,1,64,512]{3,2,1,0:T(8,128)(2,1)} %copy-done.7) | copy-start | bytes 3145732
  84.3 0.8 collective-permute-start.7
  86.9 11.8 %all-to-all-start.3 = ((f32[32,8,128]{2,1,0:T(8,128)}), f32[32,8,128]{2,1,0:T(8,128)S(1)}, u32[]{:S(2)}, u32[]{:S(2)}) async-start(f32[32,8,128]{2,1,0:T(8,128)} %shard_map.57), calls=%async_computation.3 | async-start | bytes 262144 | tf_op jit(solution)/shard_map/all_to_all | solution.py:67
  91.2 12.2 %collective-permute-start.14 = (bf16[16,1,64,512]{3,2,1,0:T(8,128)(2,1)S(1)}, bf16[16,1,64,512]{3,2,1,0:T(8,128)(2,1)}, u32[]{:S(2)}, u32[]{:S(2)}) collective-permute-start(bf16[16,1,64,512]{3,2,1,0:T(8,128)(2,1)S(1)} %copy-done.8), channel_id=1, source_target_pairs={{0,16},{16,0},{1,17},{17,1},{2,18},{18,2},{3,19},{19,3},{4,20},{20... | collective-permute-start | bytes 3145736 | tf_op jit(solution)/shard_map/ppermute | solution.py:39
  98.7 2.2 %copy-start.2 = (bf16[2,16,64,1024]{3,2,1,0:T(8,128)(2,1)S(1)}, bf16[2,16,64,1024]{3,2,1,0:T(8,128)(2,1)}, u32[]{:S(2)}) copy-start(bf16[2,16,64,1024]{3,2,1,0:T(8,128)(2,1)} %copy-done) | copy-start | bytes 12582916
  101.9 3.2 %collective-permute-start.13 = (bf16[16,1,64,512]{3,2,1,0:T(8,128)(2,1)}, bf16[16,1,64,512]{3,2,1,0:T(8,128)(2,1)S(1)}, u32[]{:S(2)}, u32[]{:S(2)}) collective-permute-start(bf16[16,1,64,512]{3,2,1,0:T(8,128)(2,1)} %collective-permute-done.8.refs_0_), channel_id=1, source_target_pairs={{0,16},{16,0},{1,17},{17,1},{2,18},{18,2},{3,19},{19,3},{4,20},{20... | collective-permute-start | bytes 3145736 | tf_op jit(solution)/shard_map/ppermute | solution.py:39
  102.7 22.1 %collective-permute-start.16 = (bf16[16,64,512]{2,1,0:T(8,128)(2,1)S(1)}, bf16[16,64,512]{2,1,0:T(8,128)(2,1)S(1)}, u32[]{:S(2)}, u32[]{:S(2)}) collective-permute-start(bf16[16,64,512]{2,1,0:T(8,128)(2,1)S(1)} %shard_map.62.inverse_own_ref), channel_id=1, source_target_pairs={{0,16},{16,0},{1,17},{17,1},{2,18},{18,2},{3,19},{19,3},{4,20},{20... | collective-permute-start | bytes 3145736 | tf_op jit(solution)/shard_map/ppermute | solution.py:39
  102.8 5.7 %collective-permute-start.12 = (f32[32,1024]{1,0:T(8,128)S(1)}, f32[32,1024]{1,0:T(8,128)S(1)}, u32[]{:S(2)}, u32[]{:S(2)}) collective-permute-start(f32[32,1024]{1,0:T(8,128)S(1)} %shard_map.58.base_ref.state_ref), channel_id=1, source_target_pairs={{160,96},{161,97},{162,98},{163,99},{164,100},{165,101},{166,102},... | collective-permute-start | bytes 393224 | tf_op jit(solution)/shard_map/ppermute | solution.py:35
  105.1 1.0 copy-start.9
  106.1 3.4 %copy-start.3 = (bf16[2,16,64,1024]{3,2,1,0:T(8,128)(2,1)S(1)}, bf16[2,16,64,1024]{3,2,1,0:T(8,128)(2,1)}, u32[]{:S(2)}) copy-start(bf16[2,16,64,1024]{3,2,1,0:T(8,128)(2,1)} %copy-done) | copy-start | bytes 12582916
  124.0 0.7 collective-permute-start.15
  140.9 25.4 %collective-permute-start.17 = (bf16[32,1024]{1,0:T(8,128)(2,1)S(1)}, bf16[32,1024]{1,0:T(8,128)(2,1)S(1)}, u32[]{:S(2)}, u32[]{:S(2)}) collective-permute-start(bf16[32,1024]{1,0:T(8,128)(2,1)S(1)} %get-tuple-element.40), channel_id=1, source_target_pairs={{32,0},{96,64},{160,128},{192,160},{224,192},{33,1},{97,65},{161,1... | collective-permute-start | bytes 196616 | tf_op jit(solution)/shard_map/ppermute | solution.py:35
  185.5 4.7 %collective-permute-start.18 = (bf16[16,32,1024]{2,1,0:T(8,128)(2,1)S(1)}, bf16[16,32,1024]{2,1,0:T(8,128)(2,1)S(1)}, u32[]{:S(2)}, u32[]{:S(2)}) collective-permute-start(bf16[16,32,1024]{2,1,0:T(8,128)(2,1)S(1)} %all_to_all.38.own_ref), channel_id=1, source_target_pairs={{0,16},{16,0},{1,17},{17,1},{2,18},{18,2},{3,19},{19,3},{4,20},{20... | collective-permute-start | bytes 3145736 | tf_op jit(solution)/shard_map/ppermute | solution.py:39

commit v2 on v1

--- a/solution.py
+++ b/solution.py
@@ -387,8 +387,8 @@
     state = step(first_state, near, [own])
     state = step(state, hop(state, 1, (6,)), [own])
 
-    pair_state, next_first, beside = lax.optimization_barrier(
-        (state, next_first, around(inverse_line, SIDE))
+    pair_state, next_first, next_last, beside = lax.optimization_barrier(
+        (state, next_first, next_last, around(inverse_line, SIDE))
     )
     far = hop(pair_state, 2, (5,))
     inverse_mine = lined(inverse_line, beside, SIDE)

time: 197 us -> 194 us (0.985)
  blocking collectives: 56.8 us -> 67.8 us
  waiting for transfers between devices: 62.2 us -> 55.3 us
  starting transfers between devices: 41.3 us -> 36.8 us
  local copies, waits for them, and re-layouts: 10.9 us -> 8.74 us
    all_to_all x3 -> x4, blocking collectives: 37.7 us -> 48.7 us  [to_devices(): return lax.all_to_all(value, ('row', 'col'), 0, 0, tiled=True)]
    all_to_all x2 -> x1, waiting for transfers between devices: 9.78 us -> 2.76 us  [to_devices(): return lax.all_to_all(value, ('row', 'col'), 0, 0, tiled=True)]
    all_to_all x2 -> x1, starting transfers between devices: 8.55 us -> 4.27 us  [to_devices(): return lax.all_to_all(value, ('row', 'col'), 0, 0, tiled=True)]
    unnamed x22, local copies, waits for them, and re-layouts: 9.7 us -> 7.58 us
  transfers between devices with their start and end apart: 22 -> 21, of which waited for: 8 -> 8; matrix products, arithmetic and copies ran while one was open for 0% -> 0% of each run, Pallas kernels for 7% -> 7%
where the time goes in v2:
time: 194 us; the launch traced here: 193 us
  blocking collectives  67.8 us (35%)
  waiting for transfers between devices  55.3 us (29%)
  starting transfers between devices  36.8 us (19%)
  Pallas kernels  23.8 us (12%)
  local copies, waits for them, and re-layouts  8.74 us (5%)
    all_to_all x4, blocking collectives, to_devices(): return lax.all_to_all(value, ('row', 'col'), 0, 0, tiled=True)  48.7 us
    ppermute x7, waiting for transfers between devices, hop(): lax.ppermute(value, 'days', [(source, source - steps) for source in sourc...  23.4 us
    ppermute x6, waiting for transfers between devices, around(): lax.ppermute(value, 'col', [(chip, chip + ((chip // stride + turn) % SIDE...  21 us
    all_to_all x1, blocking collectives, to_chips(): return lax.all_to_all(value, 'col', 0, 0, tiled=True)  19.1 us
    pallas_call x11, Pallas kernels, call(): pl.pallas_call(body, out_shape=outs if single else tuple(outs), in_specs=...  14 us
    ppermute x6, starting transfers between devices, around(): lax.ppermute(value, 'col', [(chip, chip + ((chip // stride + turn) % SIDE...  10.4 us
    ppermute x6, starting transfers between devices, other_core(): return lax.ppermute(value, 'row', [(0, 1), (1, 0)])  8.16 us
    ppermute x6, waiting for transfers between devices, other_core(): return lax.ppermute(value, 'row', [(0, 1), (1, 0)])  7.77 us
  transfers between devices with their start and end apart: 21, of which 8 were waited for; matrix products, arithmetic and copies ran while one was open for 0% of the time, Pallas kernels for 7%

profile of v2, /device:TPU:1, one launch (start us, length us, event | category | flops | bytes accessed | tf_op | source)
XLA Modules:
  0.0 193.5 jit_solution(7462385082861842345)
XLA Ops:
  0.6 0.9 copy-done.4
  1.5 0.1 shard_map.50
  1.7 1.4 copy-done.3
  3.0 7.7 %all-to-all-start = ((bf16[16,2,64,512]{3,2,1,0:T(8,128)(2,1)}), bf16[16,2,64,512]{3,2,1,0:T(8,128)(2,1)S(1)}, u32[]{:S(2)}, u32[]{:S(2)}) async-start(bf16[16,2,64,512]{3,2,1,0:T(8,128)(2,1)} %copy-done.3), calls=%async_computation | async-start | bytes 4194304 | tf_op jit(solution)/shard_map/all_to_all | solution.py:63
  10.8 1.0 collective-permute-start.3
  11.9 1.7 collective-permute-start
  13.6 2.4 %collective-permute-start.1 = (bf16[1,64,512]{2,1,0:T(8,128)(2,1)S(1)}, bf16[1,64,512]{2,1,0:T(8,128)(2,1)S(1)}, u32[]{:S(2)}, u32[]{:S(2)}) collective-permute-start(bf16[1,64,512]{2,1,0:T(8,128)(2,1)S(1)} %get-tuple-element.52.refs_0_), channel_id=1, source_target_pairs={{0,2},{1,3},{2,0},{3,1},{4,6},{5,7},{6,4},{7,5},{8,10},{9,11},{10,... | collective-permute-start | bytes 196616 | tf_op jit(solution)/shard_map/ppermute | solution.py:45
  16.0 1.2 collective-permute-start.2
  17.2 21.0 %collective-permute-done.refs_1_ = bf16[1,64,512]{2,1,0:T(8,128)(2,1)S(1)} collective-permute-done((bf16[1,64,512]{2,1,0:T(8,128)(2,1)S(1)}, bf16[1,64,512]{2,1,0:T(8,128)(2,1)S(1)}, u32[]{:S(2)}, u32[]{:S(2)}) %collective-permute-start) | collective-permute-done | bytes 65568 | tf_op jit(solution)/shard_map/ppermute | solution.py:45
  38.1 0.0 collective-permute-done.1.refs_2_
  38.3 0.3 all-to-all-done.refs_0_.refs_2_
  38.7 1.1 fusion.1
  39.8 3.5 %collective-permute-start.4 = (bf16[16,2,64,512]{3,2,1,0:T(8,128)(2,1)S(1)}, bf16[16,2,64,512]{3,2,1,0:T(8,128)(2,1)S(1)}, u32[]{:S(2)}, u32[]{:S(2)}) collective-permute-start(bf16[16,2,64,512]{3,2,1,0:T(8,128)(2,1)S(1)} %all-to-all-done.refs_0_.refs_2_), channel_id=1, source_target_pairs={{0,16},{16,0},{1,17},{17,1},{2,18},{18,2},{3,19},{19,3},{4,20},{20... | collective-permute-start | bytes 6291464 | tf_op jit(solution)/shard_map/ppermute | solution.py:39
  43.2 0.7 collective-permute-start.6
  44.0 3.1 %collective-permute-done.4.refs_1_.refs_3_ = bf16[16,2,64,512]{3,2,1,0:T(8,128)(2,1)S(1)} collective-permute-done((bf16[16,2,64,512]{3,2,1,0:T(8,128)(2,1)S(1)}, bf16[16,2,64,512]{3,2,1,0:T(8,128)(2,1)S(1)}, u32[]{:S(2)}, u32[]{:S(2)}) %collective-permute-start.4) | collective-permute-done | bytes 2097184 | tf_op jit(solution)/shard_map/ppermute | solution.py:39
  47.0 0.7 shard_map.52.factor_ref.refs_0_.refs_1_
  47.7 1.3 shard_map.53
  49.0 14.1 %all_to_all.35.packed_ref = f32[32,16,128]{2,1,0:T(8,128)S(1)} all-to-all(f32[32,16,128]{2,1,0:T(8,128)S(1)} %shard_map.53), channel_id=1, replica_groups=mesh['days'=8,'row'=2,'col'=16] {'row','col'}, dimensions={0} | all-to-all | bytes 524288 | tf_op jit(solution)/shard_map/all_to_all | solution.py:67
  63.1 0.9 shard_map.54.base_ref
  64.0 0.7 collective-permute-start.5
  64.7 1.0 copy-done.6
  65.7 1.7 collective-permute-start.8
  67.4 1.8 shard_map.55
  69.1 4.3 %all-to-all-start.2 = ((f32[32,8,128]{2,1,0:T(8,128)}), f32[32,8,128]{2,1,0:T(8,128)S(1)}, u32[]{:S(2)}, u32[]{:S(2)}) async-start(f32[32,8,128]{2,1,0:T(8,128)} %shard_map.55), calls=%async_computation.2 | async-start | bytes 262144 | tf_op jit(solution)/shard_map/all_to_all | solution.py:67
  73.4 1.5 collective-permute-start.9
  74.9 2.4 %collective-permute-start.10 = (bf16[4,64,512]{2,1,0:T(8,128)(2,1)S(1)}, bf16[4,64,512]{2,1,0:T(8,128)(2,1)S(1)}, u32[]{:S(2)}, u32[]{:S(2)}) collective-permute-start(bf16[4,64,512]{2,1,0:T(8,128)(2,1)S(1)} %shard_map.51.refs_0_), channel_id=1, source_target_pairs={{0,8},{1,9},{2,10},{3,11},{4,12},{5,13},{6,14},{7,15},{8,0},{9,1},... | collective-permute-start | bytes 786440 | tf_op jit(solution)/shard_map/ppermute | solution.py:45
  77.3 1.2 collective-permute-start.11
  78.5 2.8 %all-to-all-done.2.packed_ref = f32[32,8,128]{2,1,0:T(8,128)S(1)} async-done(((f32[32,8,128]{2,1,0:T(8,128)}), f32[32,8,128]{2,1,0:T(8,128)S(1)}, u32[]{:S(2)}, u32[]{:S(2)}) %all-to-all-start.2) | async-done | bytes 131104 | tf_op jit(solution)/shard_map/all_to_all | solution.py:67
  81.2 2.2 %copy-done.1 = bf16[2,16,64,1024]{3,2,1,0:T(8,128)(2,1)S(1)} copy-done((bf16[2,16,64,1024]{3,2,1,0:T(8,128)(2,1)S(1)}, bf16[2,16,64,1024]{3,2,1,0:T(8,128)(2,1)}, u32[]{:S(2)}) %copy-start.1) | copy-done | bytes 4194328
  83.4 0.9 shard_map.56.base_ref
  84.3 0.7 collective-permute-start.7
  85.0 0.0 collective-permute-done.7.rows_ref
  85.0 1.1 shard_map.57
  86.1 11.0 %all_to_all.36.packed_ref = f32[32,8,128]{2,1,0:T(8,128)S(1)} all-to-all(f32[32,8,128]{2,1,0:T(8,128)S(1)} %shard_map.57), channel_id=1, replica_groups=mesh['days'=8,'row'=2,'col'=16] {'row','col'}, dimensions={0} | all-to-all | bytes 262144 | tf_op jit(solution)/shard_map/all_to_all | solution.py:67
  97.1 0.9 shard_map.58.base_ref.state_ref
  98.0 0.0 collective-permute-done.9.refs_1_
  98.1 0.0 collective-permute-done.8.refs_0_
  98.1 0.7 collective-permute-start.13
  98.7 0.2 collective-permute-start.14
  98.9 0.1 shard_map.62.inverse_own_ref
  99.0 0.4 collective-permute-start.16
  99.4 0.7 collective-permute-start.12
  100.1 1.1 collective-permute-done.13.refs_1_
  101.2 1.3 collective-permute-done.14.refs_3_
  102.5 1.1 copy-done.9
  103.6 2.4 %shard_map.59.refs_0_.next_ref = bf16[2,16,64,1024]{3,2,1,0:T(8,128)(2,1)S(1)} custom-call(bf16[16,1,64,512]{3,2,1,0:T(8,128)(2,1)} %collective-permute-done.8.refs_0_, bf16[16,1,64,512]{3,2,1,0:T(8,128)(2,1)} %copy-done.8, bf16[16,1,64,512]{3,2,1,0:T(8,128)(2,1)} %copy-done.6, bf16[16,1,64,512]{3,2,1,0:T(8,128)(2,1)} %copy-done.9), custom_call_target="tpu_custom_call" | custom-call | tf_op jit(solution)/shard_map/pallas_call | solution.py:184
  106.0 0.0 collective-permute-done.12.rows_ref
  106.0 1.1 copy-done.2
  107.0 1.8 shard_map.60
  108.9 11.1 %all_to_all.37.packed_ref = f32[32,8,128]{2,1,0:T(8,128)S(1)} all-to-all(f32[32,8,128]{2,1,0:T(8,128)S(1)} %shard_map.60), channel_id=1, replica_groups=mesh['days'=8,'row'=2,'col'=16] {'row','col'}, dimensions={0} | all-to-all | bytes 262144 | tf_op jit(solution)/shard_map/all_to_all | solution.py:67
  119.9 1.6 shard_map.61
  121.6 0.7 collective-permute-start.15
  122.3 0.0 collective-permute-done.16.inverse_other_ref
  122.3 0.0 collective-permute-done.15.far_ref
  122.3 1.9 shard_map.63
  124.2 12.6 %all_to_all.38.packed_ref = f32[32,16,128]{2,1,0:T(8,128)S(1)} all-to-all(f32[32,16,128]{2,1,0:T(8,128)S(1)} %shard_map.63), channel_id=1, replica_groups=mesh['days'=8,'row'=2,'col'=16] {'row','col'}, dimensions={0} | all-to-all | bytes 524288 | tf_op jit(solution)/shard_map/all_to_all | solution.py:67
  136.7 1.7 shard_map.64
  138.4 1.3 collective-permute-start.17
  139.7 23.4 %collective-permute-done.17.arrived_ref = bf16[32,1024]{1,0:T(8,128)(2,1)S(1)} collective-permute-done((bf16[32,1024]{1,0:T(8,128)(2,1)S(1)}, bf16[32,1024]{1,0:T(8,128)(2,1)S(1)}, u32[]{:S(2)}, u32[]{:S(2)}) %collective-permute-start.17) | collective-permute-done | bytes 65568 | tf_op jit(solution)/shard_map/ppermute | solution.py:35
  163.1 0.1 shard_map.65
  163.2 19.1 %all_to_all.39.own_ref = bf16[16,32,1024]{2,1,0:T(8,128)(2,1)S(1)} all-to-all(bf16[16,32,1024]{2,1,0:T(8,128)(2,1)S(1)} %shard_map.65), channel_id=1, replica_groups=mesh['days'=8,'row'=2,'col'=16] {'col'}, dimensions={0} | all-to-all | bytes 2097152 | tf_op jit(solution)/shard_map/all_to_all | solution.py:63
  182.3 2.4 %collective-permute-start.18 = (bf16[16,32,1024]{2,1,0:T(8,128)(2,1)S(1)}, bf16[16,32,1024]{2,1,0:T(8,128)(2,1)S(1)}, u32[]{:S(2)}, u32[]{:S(2)}) collective-permute-start(bf16[16,32,1024]{2,1,0:T(8,128)(2,1)S(1)} %all_to_all.39.own_ref), channel_id=1, source_target_pairs={{0,16},{16,0},{1,17},{17,1},{2,18},{18,2},{3,19},{19,3},{4,20},{20... | collective-permute-start | bytes 3145736 | tf_op jit(solution)/shard_map/ppermute | solution.py:39
  184.7 2.3 %collective-permute-done.18.other_ref = bf16[16,32,1024]{2,1,0:T(8,128)(2,1)S(1)} collective-permute-done((bf16[16,32,1024]{2,1,0:T(8,128)(2,1)S(1)}, bf16[16,32,1024]{2,1,0:T(8,128)(2,1)S(1)}, u32[]{:S(2)}, u32[]{:S(2)}) %collective-permute-start.18) | collective-permute-done | bytes 1048608 | tf_op jit(solution)/shard_map/ppermute | solution.py:39
  187.0 6.5 %shard_map.66 = (bf16[2,64,512]{2,1,0:T(8,128)(2,1)}, bf16[2,64,512]{2,1,0:T(8,128)(2,1)}) custom-call(bf16[16,32,1024]{2,1,0:T(8,128)(2,1)S(1)} %all_to_all.39.own_ref, bf16[16,32,1024]{2,1,0:T(8,128)(2,1)S(1)} %collective-permute-done.18.other_ref, bf16[2,16,64,1024]{3,2,1,0:T(8,128)(2,1)S(1)} %copy-done.2, ...), custom_call_target="tpu_custom_call" | custom-call | tf_op jit(solution)/shard_map/pallas_call | solution.py:423
  (29 shorter events, 0.2 us)
Async XLA Ops:
  0.6 0.9 copy-start.4
  1.7 1.4 copy-start.3
  3.0 7.7 %copy-start.5 = (bf16[2,64,512]{2,1,0:T(8,128)(2,1)S(1)}, bf16[2,64,512]{2,1,0:T(8,128)(2,1)}, u32[]{:S(2)}) copy-start(bf16[2,64,512]{2,1,0:T(8,128)(2,1)} %param.3) | copy-start | bytes 393220
  3.0 7.7 %copy-start.10 = (bf16[64,512]{1,0:T(8,128)(2,1)S(1)}, bf16[64,512]{1,0:T(8,128)(2,1)}, u32[]{:S(2)}) copy-start(bf16[64,512]{1,0:T(8,128)(2,1)} %param.5) | copy-start | bytes 196612
  3.0 35.6 %all-to-all-start = ((bf16[16,2,64,512]{3,2,1,0:T(8,128)(2,1)}), bf16[16,2,64,512]{3,2,1,0:T(8,128)(2,1)S(1)}, u32[]{:S(2)}, u32[]{:S(2)}) async-start(bf16[16,2,64,512]{3,2,1,0:T(8,128)(2,1)} %copy-done.3), calls=%async_computation | async-start | bytes 4194304 | tf_op jit(solution)/shard_map/all_to_all | solution.py:63
  10.8 27.4 %collective-permute-start.3 = (bf16[3,64,512]{2,1,0:T(8,128)(2,1)S(1)}, bf16[3,64,512]{2,1,0:T(8,128)(2,1)S(1)}, u32[]{:S(2)}, u32[]{:S(2)}) collective-permute-start(bf16[3,64,512]{2,1,0:T(8,128)(2,1)S(1)} %pad_maximum_fusion), channel_id=1, source_target_pairs={{0,16},{16,0},{1,17},{17,1},{2,18},{18,2},{3,19},{19,3},{4,20},{20... | collective-permute-start | bytes 589832 | tf_op jit(solution)/shard_map/ppermute | solution.py:39
  11.9 26.3 %collective-permute-start = (bf16[1,64,512]{2,1,0:T(8,128)(2,1)S(1)}, bf16[1,64,512]{2,1,0:T(8,128)(2,1)S(1)}, u32[]{:S(2)}, u32[]{:S(2)}) collective-permute-start(bf16[1,64,512]{2,1,0:T(8,128)(2,1)S(1)} %get-tuple-element.52.refs_0_), channel_id=1, source_target_pairs={{0,1},{1,2},{2,3},{3,0},{4,5},{5,6},{6,7},{7,4},{8,9},{9,10},{10,1... | collective-permute-start | bytes 196616 | tf_op jit(solution)/shard_map/ppermute | solution.py:45
  13.6 24.5 %collective-permute-start.1 = (bf16[1,64,512]{2,1,0:T(8,128)(2,1)S(1)}, bf16[1,64,512]{2,1,0:T(8,128)(2,1)S(1)}, u32[]{:S(2)}, u32[]{:S(2)}) collective-permute-start(bf16[1,64,512]{2,1,0:T(8,128)(2,1)S(1)} %get-tuple-element.52.refs_0_), channel_id=1, source_target_pairs={{0,2},{1,3},{2,0},{3,1},{4,6},{5,7},{6,4},{7,5},{8,10},{9,11},{10,... | collective-permute-start | bytes 196616 | tf_op jit(solution)/shard_map/ppermute | solution.py:45
  16.0 22.1 %collective-permute-start.2 = (bf16[1,64,512]{2,1,0:T(8,128)(2,1)S(1)}, bf16[1,64,512]{2,1,0:T(8,128)(2,1)S(1)}, u32[]{:S(2)}, u32[]{:S(2)}) collective-permute-start(bf16[1,64,512]{2,1,0:T(8,128)(2,1)S(1)} %get-tuple-element.52.refs_0_), channel_id=1, source_target_pairs={{0,3},{1,0},{2,1},{3,2},{4,7},{5,4},{6,5},{7,6},{8,11},{9,8},{10,9... | collective-permute-start | bytes 196616 | tf_op jit(solution)/shard_map/ppermute | solution.py:45
  39.8 7.2 %collective-permute-start.4 = (bf16[16,2,64,512]{3,2,1,0:T(8,128)(2,1)S(1)}, bf16[16,2,64,512]{3,2,1,0:T(8,128)(2,1)S(1)}, u32[]{:S(2)}, u32[]{:S(2)}) collective-permute-start(bf16[16,2,64,512]{3,2,1,0:T(8,128)(2,1)S(1)} %all-to-all-done.refs_0_.refs_2_), channel_id=1, source_target_pairs={{0,16},{16,0},{1,17},{17,1},{2,18},{18,2},{3,19},{19,3},{4,20},{20... | collective-permute-start | bytes 6291464 | tf_op jit(solution)/shard_map/ppermute | solution.py:39
  43.2 21.4 %collective-permute-start.6 = (bf16[16,1,64,512]{3,2,1,0:T(8,128)(2,1)S(1)}, bf16[16,1,64,512]{3,2,1,0:T(8,128)(2,1)S(1)}, u32[]{:S(2)}, u32[]{:S(2)}) collective-permute-start(bf16[16,1,64,512]{3,2,1,0:T(8,128)(2,1)S(1)} %get-tuple-element.28), channel_id=1, source_target_pairs={{64,32},{128,96},{65,33},{129,97},{66,34},{130,98},{67,35},{131,99... | collective-permute-start | bytes 3145736 | tf_op jit(solution)/shard_map/ppermute | solution.py:35
  47.7 19.6 %copy-start = (bf16[2,16,64,1024]{3,2,1,0:T(8,128)(2,1)}, bf16[2,16,64,1024]{3,2,1,0:T(8,128)(2,1)S(1)}, u32[]{:S(2)}) copy-start(bf16[2,16,64,1024]{3,2,1,0:T(8,128)(2,1)S(1)} %shard_map.52.factor_ref.refs_0_.refs_1_) | copy-start | bytes 12582916
  64.0 0.7 collective-permute-start.5
  64.7 1.0 copy-start.6
  65.7 32.4 %collective-permute-start.8 = (bf16[16,1,64,512]{3,2,1,0:T(8,128)(2,1)}, bf16[16,1,64,512]{3,2,1,0:T(8,128)(2,1)}, u32[]{:S(2)}, u32[]{:S(2)}) collective-permute-start(bf16[16,1,64,512]{3,2,1,0:T(8,128)(2,1)} %get-tuple-element.30), channel_id=1, source_target_pairs={{64,32},{128,96},{65,33},{129,97},{66,34},{130,98},{67,35},{131,99... | collective-permute-start | bytes 3145736 | tf_op jit(solution)/shard_map/ppermute | solution.py:35
  69.1 12.1 %all-to-all-start.2 = ((f32[32,8,128]{2,1,0:T(8,128)}), f32[32,8,128]{2,1,0:T(8,128)S(1)}, u32[]{:S(2)}, u32[]{:S(2)}) async-start(f32[32,8,128]{2,1,0:T(8,128)} %shard_map.55), calls=%async_computation.2 | async-start | bytes 262144 | tf_op jit(solution)/shard_map/all_to_all | solution.py:67
  73.4 24.6 %collective-permute-start.9 = (bf16[4,64,512]{2,1,0:T(8,128)(2,1)S(1)}, bf16[4,64,512]{2,1,0:T(8,128)(2,1)S(1)}, u32[]{:S(2)}, u32[]{:S(2)}) collective-permute-start(bf16[4,64,512]{2,1,0:T(8,128)(2,1)S(1)} %shard_map.51.refs_0_), channel_id=1, source_target_pairs={{0,4},{1,5},{2,6},{3,7},{4,8},{5,9},{6,10},{7,11},{8,12},{9,13},{1... | collective-permute-start | bytes 786440 | tf_op jit(solution)/shard_map/ppermute | solution.py:45
  74.9 23.2 %collective-permute-start.10 = (bf16[4,64,512]{2,1,0:T(8,128)(2,1)S(1)}, bf16[4,64,512]{2,1,0:T(8,128)(2,1)S(1)}, u32[]{:S(2)}, u32[]{:S(2)}) collective-permute-start(bf16[4,64,512]{2,1,0:T(8,128)(2,1)S(1)} %shard_map.51.refs_0_), channel_id=1, source_target_pairs={{0,8},{1,9},{2,10},{3,11},{4,12},{5,13},{6,14},{7,15},{8,0},{9,1},... | collective-permute-start | bytes 786440 | tf_op jit(solution)/shard_map/ppermute | solution.py:45
  77.3 20.7 %collective-permute-start.11 = (bf16[4,64,512]{2,1,0:T(8,128)(2,1)S(1)}, bf16[4,64,512]{2,1,0:T(8,128)(2,1)S(1)}, u32[]{:S(2)}, u32[]{:S(2)}) collective-permute-start(bf16[4,64,512]{2,1,0:T(8,128)(2,1)S(1)} %shard_map.51.refs_0_), channel_id=1, source_target_pairs={{0,12},{1,13},{2,14},{3,15},{4,0},{5,1},{6,2},{7,3},{8,4},{9,5},{1... | collective-permute-start | bytes 786440 | tf_op jit(solution)/shard_map/ppermute | solution.py:45
  81.2 2.2 %copy-start.1 = (bf16[2,16,64,1024]{3,2,1,0:T(8,128)(2,1)S(1)}, bf16[2,16,64,1024]{3,2,1,0:T(8,128)(2,1)}, u32[]{:S(2)}) copy-start(bf16[2,16,64,1024]{3,2,1,0:T(8,128)(2,1)} %copy-done) | copy-start | bytes 12582916
  84.3 0.7 collective-permute-start.7
  97.1 1.6 copy-start.7
  98.1 3.2 %collective-permute-start.13 = (bf16[16,1,64,512]{3,2,1,0:T(8,128)(2,1)}, bf16[16,1,64,512]{3,2,1,0:T(8,128)(2,1)S(1)}, u32[]{:S(2)}, u32[]{:S(2)}) collective-permute-start(bf16[16,1,64,512]{3,2,1,0:T(8,128)(2,1)} %collective-permute-done.8.refs_0_), channel_id=1, source_target_pairs={{0,16},{16,0},{1,17},{17,1},{2,18},{18,2},{3,19},{19,3},{4,20},{20... | collective-permute-start | bytes 3145736 | tf_op jit(solution)/shard_map/ppermute | solution.py:39
  98.7 3.8 %collective-permute-start.14 = (bf16[16,1,64,512]{3,2,1,0:T(8,128)(2,1)S(1)}, bf16[16,1,64,512]{3,2,1,0:T(8,128)(2,1)S(1)}, u32[]{:S(2)}, u32[]{:S(2)}) collective-permute-start(bf16[16,1,64,512]{3,2,1,0:T(8,128)(2,1)S(1)} %copy-done.7), channel_id=1, source_target_pairs={{0,16},{16,0},{1,17},{17,1},{2,18},{18,2},{3,19},{19,3},{4,20},{20... | collective-permute-start | bytes 3145736 | tf_op jit(solution)/shard_map/ppermute | solution.py:39
  99.0 23.2 %collective-permute-start.16 = (bf16[16,64,512]{2,1,0:T(8,128)(2,1)S(1)}, bf16[16,64,512]{2,1,0:T(8,128)(2,1)S(1)}, u32[]{:S(2)}, u32[]{:S(2)}) collective-permute-start(bf16[16,64,512]{2,1,0:T(8,128)(2,1)S(1)} %shard_map.62.inverse_own_ref), channel_id=1, source_target_pairs={{0,16},{16,0},{1,17},{17,1},{2,18},{18,2},{3,19},{19,3},{4,20},{20... | collective-permute-start | bytes 3145736 | tf_op jit(solution)/shard_map/ppermute | solution.py:39
  99.4 6.5 %collective-permute-start.12 = (f32[32,1024]{1,0:T(8,128)S(1)}, f32[32,1024]{1,0:T(8,128)S(1)}, u32[]{:S(2)}, u32[]{:S(2)}) collective-permute-start(f32[32,1024]{1,0:T(8,128)S(1)} %shard_map.58.base_ref.state_ref), channel_id=1, source_target_pairs={{160,96},{161,97},{162,98},{163,99},{164,100},{165,101},{166,102},... | collective-permute-start | bytes 393224 | tf_op jit(solution)/shard_map/ppermute | solution.py:35
  101.2 1.3 copy-start.8
  102.5 1.1 copy-start.9
  103.6 3.4 %copy-start.2 = (bf16[2,16,64,1024]{3,2,1,0:T(8,128)(2,1)S(1)}, bf16[2,16,64,1024]{3,2,1,0:T(8,128)(2,1)}, u32[]{:S(2)}) copy-start(bf16[2,16,64,1024]{3,2,1,0:T(8,128)(2,1)} %copy-done) | copy-start | bytes 12582916
  121.6 0.7 collective-permute-start.15
  138.4 24.7 %collective-permute-start.17 = (bf16[32,1024]{1,0:T(8,128)(2,1)S(1)}, bf16[32,1024]{1,0:T(8,128)(2,1)S(1)}, u32[]{:S(2)}, u32[]{:S(2)}) collective-permute-start(bf16[32,1024]{1,0:T(8,128)(2,1)S(1)} %get-tuple-element.42), channel_id=1, source_target_pairs={{32,0},{96,64},{160,128},{192,160},{224,192},{33,1},{97,65},{161,1... | collective-permute-start | bytes 196616 | tf_op jit(solution)/shard_map/ppermute | solution.py:35
  182.3 4.7 %collective-permute-start.18 = (bf16[16,32,1024]{2,1,0:T(8,128)(2,1)S(1)}, bf16[16,32,1024]{2,1,0:T(8,128)(2,1)S(1)}, u32[]{:S(2)}, u32[]{:S(2)}) collective-permute-start(bf16[16,32,1024]{2,1,0:T(8,128)(2,1)S(1)} %all_to_all.39.own_ref), channel_id=1, source_target_pairs={{0,16},{16,0},{1,17},{17,1},{2,18},{18,2},{3,19},{19,3},{4,20},{20... | collective-permute-start | bytes 3145736 | tf_op jit(solution)/shard_map/ppermute | solution.py:39

commit v3 on v2

--- a/solution.py
+++ b/solution.py
@@ -252,6 +252,15 @@
         out_ref[chip] = separator
 
 
+def own_rows(own_ref, factor_ref, out_ref):
+    chips, strip, nodes = own_ref.shape
+    rows = own_ref[...].reshape(chips * strip, nodes)
+    for start in range(0, chips * strip, BLOCK):
+        out_ref[start : start + BLOCK] = times(
+            rows[start : start + BLOCK], factor_ref, 1
+        ).astype(narrow)
+
+
 def inner_days(
     own_ref,
     other_ref,
@@ -270,14 +279,15 @@
     chip = lax.axis_index("col")
     _, chips, rows, nodes = factor_ref.shape
     half = nodes // 2
+    strips = other_ref[...].reshape(chips * STRIP, nodes)
+    for start in range(0, chips * STRIP, BLOCK):
+        covariance_ref[start : start + BLOCK] = times(
+            strips[start : start + BLOCK], factor_ref, 1
+        ).astype(narrow)
     for place in range(chips):
-        for ref, which in ((own_ref, core), (other_ref, 1 - core)):
+        for ref, which in ((own_ref, core), (covariance_ref, 1 - core)):
             start = pl.multiple_of(place * rows + which * STRIP, STRIP)
-            covariance_ref[pl.ds(start, STRIP)] = ref[place]
-    for start in range(0, nodes, BLOCK):
-        cross_last_ref[start : start + BLOCK] = times(
-            covariance_ref[start : start + BLOCK], factor_ref, 1
-        ).astype(narrow)
+            cross_last_ref[pl.ds(start, STRIP)] = ref[place * STRIP : (place + 1) * STRIP]
     for block in range(nodes // BLOCK):
         start = block * BLOCK
         factor_cols = factor_ref[1, :, :, start : start + BLOCK].reshape(nodes, BLOCK)
@@ -425,10 +435,11 @@
         out_shape=(block, block),
         in_specs=[vmem] * 6,
         out_specs=(vmem, vmem),
-        scratch_shapes=[square] * 3 + [pltpu.VMEM((nodes, half), narrow)],
+        scratch_shapes=[pltpu.VMEM((nodes // 2, nodes), narrow), square, square]
+        + [pltpu.VMEM((nodes, half), narrow)],
         compiler_params=params(),
     )(
-        separator,
+        call(own_rows, jax.ShapeDtypeStruct((nodes // 2, nodes), narrow), [], [separator], [own]),
         other_core(separator),
         pinned(own),
         inverse_mine,

time: 194 us -> 193 us (level)
    pallas_call x11 -> x12, Pallas kernels: 14 us -> 15.2 us  [call(): pl.pallas_call(body, out_shape=outs if single else tuple(outs), in_specs=...]
  transfers between devices with their start and end apart: 21 -> 21, of which waited for: 8 -> 8; matrix products, arithmetic and copies ran while one was open for 0% -> 0% of each run, Pallas kernels for 7% -> 8%
where the time goes in v3:
time: 193 us
  blocking collectives  67.8 us (35%)
  waiting for transfers between devices  54 us (28%)
  starting transfers between devices  36.8 us (19%)
  Pallas kernels  24.1 us (12%)
  local copies, waits for them, and re-layouts  8.74 us (5%)
    all_to_all x4, blocking collectives, to_devices(): return lax.all_to_all(value, ('row', 'col'), 0, 0, tiled=True)  48.7 us
    ppermute x7, waiting for transfers between devices, hop(): lax.ppermute(value, 'days', [(source, source - steps) for source in sourc...  23.4 us
    ppermute x6, waiting for transfers between devices, around(): lax.ppermute(value, 'col', [(chip, chip + ((chip // stride + turn) % SIDE...  21 us
    all_to_all x1, blocking collectives, to_chips(): return lax.all_to_all(value, 'col', 0, 0, tiled=True)  19.1 us
    pallas_call x12, Pallas kernels, call(): pl.pallas_call(body, out_shape=outs if single else tuple(outs), in_specs=...  15.2 us
    ppermute x6, starting transfers between devices, around(): lax.ppermute(value, 'col', [(chip, chip + ((chip // stride + turn) % SIDE...  10.4 us
    ppermute x6, starting transfers between devices, other_core(): return lax.ppermute(value, 'row', [(0, 1), (1, 0)])  8.16 us
    all_to_all x1, starting transfers between devices, to_chips(): return lax.all_to_all(value, 'col', 0, 0, tiled=True)  7.72 us
  transfers between devices with their start and end apart: 21, of which 8 were waited for; matrix products, arithmetic and copies ran while one was open for 0% of the time, Pallas kernels for 8%

profile of v3, /device:TPU:1, one launch (start us, length us, event | category | flops | bytes accessed | tf_op | source)
XLA Modules:
  0.0 192.6 jit_solution(15310404453400313454)
XLA Ops:
  0.6 0.9 copy-done.4
  1.5 0.1 shard_map.50
  1.7 1.4 copy-done.3
  3.0 7.7 %all-to-all-start = ((bf16[16,2,64,512]{3,2,1,0:T(8,128)(2,1)}), bf16[16,2,64,512]{3,2,1,0:T(8,128)(2,1)S(1)}, u32[]{:S(2)}, u32[]{:S(2)}) async-start(bf16[16,2,64,512]{3,2,1,0:T(8,128)(2,1)} %copy-done.3), calls=%async_computation | async-start | bytes 4194304 | tf_op jit(solution)/shard_map/all_to_all | solution.py:63
  10.8 1.0 collective-permute-start.3
  11.9 1.7 collective-permute-start
  13.6 2.4 %collective-permute-start.1 = (bf16[1,64,512]{2,1,0:T(8,128)(2,1)S(1)}, bf16[1,64,512]{2,1,0:T(8,128)(2,1)S(1)}, u32[]{:S(2)}, u32[]{:S(2)}) collective-permute-start(bf16[1,64,512]{2,1,0:T(8,128)(2,1)S(1)} %get-tuple-element.52.refs_0_), channel_id=1, source_target_pairs={{0,2},{1,3},{2,0},{3,1},{4,6},{5,7},{6,4},{7,5},{8,10},{9,11},{10,... | collective-permute-start | bytes 196616 | tf_op jit(solution)/shard_map/ppermute | solution.py:45
  16.0 1.2 collective-permute-start.2
  17.2 21.0 %collective-permute-done.refs_1_ = bf16[1,64,512]{2,1,0:T(8,128)(2,1)S(1)} collective-permute-done((bf16[1,64,512]{2,1,0:T(8,128)(2,1)S(1)}, bf16[1,64,512]{2,1,0:T(8,128)(2,1)S(1)}, u32[]{:S(2)}, u32[]{:S(2)}) %collective-permute-start) | collective-permute-done | bytes 65568 | tf_op jit(solution)/shard_map/ppermute | solution.py:45
  38.1 0.0 collective-permute-done.1.refs_2_
  38.1 0.0 collective-permute-done.2.refs_3_
  38.2 0.0 collective-permute-done.3
  38.3 0.3 all-to-all-done.refs_0_.refs_2_
  38.7 1.1 fusion.1
  39.8 3.5 %collective-permute-start.4 = (bf16[16,2,64,512]{3,2,1,0:T(8,128)(2,1)S(1)}, bf16[16,2,64,512]{3,2,1,0:T(8,128)(2,1)S(1)}, u32[]{:S(2)}, u32[]{:S(2)}) collective-permute-start(bf16[16,2,64,512]{3,2,1,0:T(8,128)(2,1)S(1)} %all-to-all-done.refs_0_.refs_2_), channel_id=1, source_target_pairs={{0,16},{16,0},{1,17},{17,1},{2,18},{18,2},{3,19},{19,3},{4,20},{20... | collective-permute-start | bytes 6291464 | tf_op jit(solution)/shard_map/ppermute | solution.py:39
  43.2 0.7 collective-permute-start.6
  44.0 3.1 %collective-permute-done.4.refs_1_.refs_3_ = bf16[16,2,64,512]{3,2,1,0:T(8,128)(2,1)S(1)} collective-permute-done((bf16[16,2,64,512]{3,2,1,0:T(8,128)(2,1)S(1)}, bf16[16,2,64,512]{3,2,1,0:T(8,128)(2,1)S(1)}, u32[]{:S(2)}, u32[]{:S(2)}) %collective-permute-start.4) | collective-permute-done | bytes 2097184 | tf_op jit(solution)/shard_map/ppermute | solution.py:39
  47.0 0.7 shard_map.52.factor_ref.refs_0_.refs_1_
  47.7 1.3 shard_map.53
  49.0 14.1 %all_to_all.35.packed_ref = f32[32,16,128]{2,1,0:T(8,128)S(1)} all-to-all(f32[32,16,128]{2,1,0:T(8,128)S(1)} %shard_map.53), channel_id=1, replica_groups=mesh['days'=8,'row'=2,'col'=16] {'row','col'}, dimensions={0} | all-to-all | bytes 524288 | tf_op jit(solution)/shard_map/all_to_all | solution.py:67
  63.1 0.9 shard_map.54.base_ref
  64.0 0.7 collective-permute-start.5
  64.7 0.0 collective-permute-done.5.rows_ref.near_ref
  64.7 1.0 copy-done.6
  65.7 1.7 collective-permute-start.8
  67.4 1.8 shard_map.55
  69.1 4.3 %all-to-all-start.2 = ((f32[32,8,128]{2,1,0:T(8,128)}), f32[32,8,128]{2,1,0:T(8,128)S(1)}, u32[]{:S(2)}, u32[]{:S(2)}) async-start(f32[32,8,128]{2,1,0:T(8,128)} %shard_map.55), calls=%async_computation.2 | async-start | bytes 262144 | tf_op jit(solution)/shard_map/all_to_all | solution.py:67
  73.4 1.5 collective-permute-start.9
  74.9 2.4 %collective-permute-start.10 = (bf16[4,64,512]{2,1,0:T(8,128)(2,1)S(1)}, bf16[4,64,512]{2,1,0:T(8,128)(2,1)S(1)}, u32[]{:S(2)}, u32[]{:S(2)}) collective-permute-start(bf16[4,64,512]{2,1,0:T(8,128)(2,1)S(1)} %shard_map.51.refs_0_), channel_id=1, source_target_pairs={{0,8},{1,9},{2,10},{3,11},{4,12},{5,13},{6,14},{7,15},{8,0},{9,1},... | collective-permute-start | bytes 786440 | tf_op jit(solution)/shard_map/ppermute | solution.py:45
  77.3 1.2 collective-permute-start.11
  78.5 2.8 %all-to-all-done.2.packed_ref = f32[32,8,128]{2,1,0:T(8,128)S(1)} async-done(((f32[32,8,128]{2,1,0:T(8,128)}), f32[32,8,128]{2,1,0:T(8,128)S(1)}, u32[]{:S(2)}, u32[]{:S(2)}) %all-to-all-start.2) | async-done | bytes 131104 | tf_op jit(solution)/shard_map/all_to_all | solution.py:67
  81.2 2.2 %copy-done.1 = bf16[2,16,64,1024]{3,2,1,0:T(8,128)(2,1)S(1)} copy-done((bf16[2,16,64,1024]{3,2,1,0:T(8,128)(2,1)S(1)}, bf16[2,16,64,1024]{3,2,1,0:T(8,128)(2,1)}, u32[]{:S(2)}) %copy-start.1) | copy-done | bytes 4194328
  83.4 0.9 shard_map.56.base_ref
  84.3 0.7 collective-permute-start.7
  85.0 1.1 shard_map.57
  86.1 11.0 %all_to_all.36.packed_ref = f32[32,8,128]{2,1,0:T(8,128)S(1)} all-to-all(f32[32,8,128]{2,1,0:T(8,128)S(1)} %shard_map.57), channel_id=1, replica_groups=mesh['days'=8,'row'=2,'col'=16] {'row','col'}, dimensions={0} | all-to-all | bytes 262144 | tf_op jit(solution)/shard_map/all_to_all | solution.py:67
  97.1 0.9 shard_map.58.base_ref.state_ref
  98.0 0.0 collective-permute-done.9.refs_1_
  98.0 0.0 collective-permute-done.11.refs_3_
  98.1 0.7 collective-permute-start.13
  98.7 0.2 collective-permute-start.14
  98.9 0.1 shard_map.62.inverse_own_ref
  99.0 0.4 collective-permute-start.16
  99.4 0.7 collective-permute-start.12
  100.1 1.1 collective-permute-done.13.refs_1_
  101.2 1.3 collective-permute-done.14.refs_3_
  102.5 1.1 copy-done.9
  103.6 2.4 %shard_map.59.refs_0_.next_ref = bf16[2,16,64,1024]{3,2,1,0:T(8,128)(2,1)S(1)} custom-call(bf16[16,1,64,512]{3,2,1,0:T(8,128)(2,1)} %collective-permute-done.8.refs_0_, bf16[16,1,64,512]{3,2,1,0:T(8,128)(2,1)} %copy-done.8, bf16[16,1,64,512]{3,2,1,0:T(8,128)(2,1)} %copy-done.6, bf16[16,1,64,512]{3,2,1,0:T(8,128)(2,1)} %copy-done.9), custom_call_target="tpu_custom_call" | custom-call | tf_op jit(solution)/shard_map/pallas_call | solution.py:184
  106.0 1.1 copy-done.2
  107.0 1.8 shard_map.60
  108.9 11.1 %all_to_all.37.packed_ref = f32[32,8,128]{2,1,0:T(8,128)S(1)} all-to-all(f32[32,8,128]{2,1,0:T(8,128)S(1)} %shard_map.60), channel_id=1, replica_groups=mesh['days'=8,'row'=2,'col'=16] {'row','col'}, dimensions={0} | all-to-all | bytes 262144 | tf_op jit(solution)/shard_map/all_to_all | solution.py:67
  119.9 1.6 shard_map.61
  121.6 0.7 collective-permute-start.15
  122.3 1.9 shard_map.63
  124.2 12.6 %all_to_all.38.packed_ref = f32[32,16,128]{2,1,0:T(8,128)S(1)} all-to-all(f32[32,16,128]{2,1,0:T(8,128)S(1)} %shard_map.63), channel_id=1, replica_groups=mesh['days'=8,'row'=2,'col'=16] {'row','col'}, dimensions={0} | all-to-all | bytes 524288 | tf_op jit(solution)/shard_map/all_to_all | solution.py:67
  136.7 1.7 shard_map.64
  138.4 1.3 collective-permute-start.17
  139.7 23.4 %collective-permute-done.17.arrived_ref = bf16[32,1024]{1,0:T(8,128)(2,1)S(1)} collective-permute-done((bf16[32,1024]{1,0:T(8,128)(2,1)S(1)}, bf16[32,1024]{1,0:T(8,128)(2,1)S(1)}, u32[]{:S(2)}, u32[]{:S(2)}) %collective-permute-start.17) | collective-permute-done | bytes 65568 | tf_op jit(solution)/shard_map/ppermute | solution.py:35
  163.1 0.1 shard_map.65
  163.2 19.1 %all_to_all.39.own_ref = bf16[16,32,1024]{2,1,0:T(8,128)(2,1)S(1)} all-to-all(bf16[16,32,1024]{2,1,0:T(8,128)(2,1)S(1)} %shard_map.65), channel_id=1, replica_groups=mesh['days'=8,'row'=2,'col'=16] {'col'}, dimensions={0} | all-to-all | bytes 2097152 | tf_op jit(solution)/shard_map/all_to_all | solution.py:63
  182.3 2.4 %collective-permute-start.18 = (bf16[16,32,1024]{2,1,0:T(8,128)(2,1)S(1)}, bf16[16,32,1024]{2,1,0:T(8,128)(2,1)S(1)}, u32[]{:S(2)}, u32[]{:S(2)}) collective-permute-start(bf16[16,32,1024]{2,1,0:T(8,128)(2,1)S(1)} %all_to_all.39.own_ref), channel_id=1, source_target_pairs={{0,16},{16,0},{1,17},{17,1},{2,18},{18,2},{3,19},{19,3},{4,20},{20... | collective-permute-start | bytes 3145736 | tf_op jit(solution)/shard_map/ppermute | solution.py:39
  184.7 1.2 shard_map.66.own_ref
  185.9 1.0 collective-permute-done.18.other_ref
  187.0 5.6 %shard_map.67 = (bf16[2,64,512]{2,1,0:T(8,128)(2,1)}, bf16[2,64,512]{2,1,0:T(8,128)(2,1)}) custom-call(bf16[512,1024]{1,0:T(8,128)(2,1)S(1)} %shard_map.66.own_ref, bf16[16,32,1024]{2,1,0:T(8,128)(2,1)S(1)} %collective-permute-done.18.other_ref, bf16[2,16,64,1024]{3,2,1,0:T(8,128)(2,1)S(1)} %copy-done.2, bf16[16,64,512]{2,1,0:T(8,128)(2,1)S(1)} %shard_map.62.inverse_own_ref, ...), custom_call_target="tpu_custom_call" | custom-call | tf_op jit(solution)/shard_map/pallas_call | solution.py:433
  (30 shorter events, 0.2 us)
Async XLA Ops:
  0.6 0.9 copy-start.4
  1.7 1.4 copy-start.3
  3.0 7.7 %copy-start.5 = (bf16[2,64,512]{2,1,0:T(8,128)(2,1)S(1)}, bf16[2,64,512]{2,1,0:T(8,128)(2,1)}, u32[]{:S(2)}) copy-start(bf16[2,64,512]{2,1,0:T(8,128)(2,1)} %param.3) | copy-start | bytes 393220
  3.0 7.7 %copy-start.10 = (bf16[64,512]{1,0:T(8,128)(2,1)S(1)}, bf16[64,512]{1,0:T(8,128)(2,1)}, u32[]{:S(2)}) copy-start(bf16[64,512]{1,0:T(8,128)(2,1)} %param.5) | copy-start | bytes 196612
  3.0 35.6 %all-to-all-start = ((bf16[16,2,64,512]{3,2,1,0:T(8,128)(2,1)}), bf16[16,2,64,512]{3,2,1,0:T(8,128)(2,1)S(1)}, u32[]{:S(2)}, u32[]{:S(2)}) async-start(bf16[16,2,64,512]{3,2,1,0:T(8,128)(2,1)} %copy-done.3), calls=%async_computation | async-start | bytes 4194304 | tf_op jit(solution)/shard_map/all_to_all | solution.py:63
  10.8 27.4 %collective-permute-start.3 = (bf16[3,64,512]{2,1,0:T(8,128)(2,1)S(1)}, bf16[3,64,512]{2,1,0:T(8,128)(2,1)S(1)}, u32[]{:S(2)}, u32[]{:S(2)}) collective-permute-start(bf16[3,64,512]{2,1,0:T(8,128)(2,1)S(1)} %pad_maximum_fusion), channel_id=1, source_target_pairs={{0,16},{16,0},{1,17},{17,1},{2,18},{18,2},{3,19},{19,3},{4,20},{20... | collective-permute-start | bytes 589832 | tf_op jit(solution)/shard_map/ppermute | solution.py:39
  11.9 26.3 %collective-permute-start = (bf16[1,64,512]{2,1,0:T(8,128)(2,1)S(1)}, bf16[1,64,512]{2,1,0:T(8,128)(2,1)S(1)}, u32[]{:S(2)}, u32[]{:S(2)}) collective-permute-start(bf16[1,64,512]{2,1,0:T(8,128)(2,1)S(1)} %get-tuple-element.52.refs_0_), channel_id=1, source_target_pairs={{0,1},{1,2},{2,3},{3,0},{4,5},{5,6},{6,7},{7,4},{8,9},{9,10},{10,1... | collective-permute-start | bytes 196616 | tf_op jit(solution)/shard_map/ppermute | solution.py:45
  13.6 24.5 %collective-permute-start.1 = (bf16[1,64,512]{2,1,0:T(8,128)(2,1)S(1)}, bf16[1,64,512]{2,1,0:T(8,128)(2,1)S(1)}, u32[]{:S(2)}, u32[]{:S(2)}) collective-permute-start(bf16[1,64,512]{2,1,0:T(8,128)(2,1)S(1)} %get-tuple-element.52.refs_0_), channel_id=1, source_target_pairs={{0,2},{1,3},{2,0},{3,1},{4,6},{5,7},{6,4},{7,5},{8,10},{9,11},{10,... | collective-permute-start | bytes 196616 | tf_op jit(solution)/shard_map/ppermute | solution.py:45
  16.0 22.1 %collective-permute-start.2 = (bf16[1,64,512]{2,1,0:T(8,128)(2,1)S(1)}, bf16[1,64,512]{2,1,0:T(8,128)(2,1)S(1)}, u32[]{:S(2)}, u32[]{:S(2)}) collective-permute-start(bf16[1,64,512]{2,1,0:T(8,128)(2,1)S(1)} %get-tuple-element.52.refs_0_), channel_id=1, source_target_pairs={{0,3},{1,0},{2,1},{3,2},{4,7},{5,4},{6,5},{7,6},{8,11},{9,8},{10,9... | collective-permute-start | bytes 196616 | tf_op jit(solution)/shard_map/ppermute | solution.py:45
  39.8 7.2 %collective-permute-start.4 = (bf16[16,2,64,512]{3,2,1,0:T(8,128)(2,1)S(1)}, bf16[16,2,64,512]{3,2,1,0:T(8,128)(2,1)S(1)}, u32[]{:S(2)}, u32[]{:S(2)}) collective-permute-start(bf16[16,2,64,512]{3,2,1,0:T(8,128)(2,1)S(1)} %all-to-all-done.refs_0_.refs_2_), channel_id=1, source_target_pairs={{0,16},{16,0},{1,17},{17,1},{2,18},{18,2},{3,19},{19,3},{4,20},{20... | collective-permute-start | bytes 6291464 | tf_op jit(solution)/shard_map/ppermute | solution.py:39
  43.2 21.4 %collective-permute-start.6 = (bf16[16,1,64,512]{3,2,1,0:T(8,128)(2,1)S(1)}, bf16[16,1,64,512]{3,2,1,0:T(8,128)(2,1)S(1)}, u32[]{:S(2)}, u32[]{:S(2)}) collective-permute-start(bf16[16,1,64,512]{3,2,1,0:T(8,128)(2,1)S(1)} %get-tuple-element.28), channel_id=1, source_target_pairs={{64,32},{128,96},{65,33},{129,97},{66,34},{130,98},{67,35},{131,99... | collective-permute-start | bytes 3145736 | tf_op jit(solution)/shard_map/ppermute | solution.py:35
  47.7 19.6 %copy-start = (bf16[2,16,64,1024]{3,2,1,0:T(8,128)(2,1)}, bf16[2,16,64,1024]{3,2,1,0:T(8,128)(2,1)S(1)}, u32[]{:S(2)}) copy-start(bf16[2,16,64,1024]{3,2,1,0:T(8,128)(2,1)S(1)} %shard_map.52.factor_ref.refs_0_.refs_1_) | copy-start | bytes 12582916
  64.0 0.7 collective-permute-start.5
  64.7 1.0 copy-start.6
  65.7 32.4 %collective-permute-start.8 = (bf16[16,1,64,512]{3,2,1,0:T(8,128)(2,1)}, bf16[16,1,64,512]{3,2,1,0:T(8,128)(2,1)}, u32[]{:S(2)}, u32[]{:S(2)}) collective-permute-start(bf16[16,1,64,512]{3,2,1,0:T(8,128)(2,1)} %get-tuple-element.30), channel_id=1, source_target_pairs={{64,32},{128,96},{65,33},{129,97},{66,34},{130,98},{67,35},{131,99... | collective-permute-start | bytes 3145736 | tf_op jit(solution)/shard_map/ppermute | solution.py:35
  69.1 12.1 %all-to-all-start.2 = ((f32[32,8,128]{2,1,0:T(8,128)}), f32[32,8,128]{2,1,0:T(8,128)S(1)}, u32[]{:S(2)}, u32[]{:S(2)}) async-start(f32[32,8,128]{2,1,0:T(8,128)} %shard_map.55), calls=%async_computation.2 | async-start | bytes 262144 | tf_op jit(solution)/shard_map/all_to_all | solution.py:67
  73.4 24.6 %collective-permute-start.9 = (bf16[4,64,512]{2,1,0:T(8,128)(2,1)S(1)}, bf16[4,64,512]{2,1,0:T(8,128)(2,1)S(1)}, u32[]{:S(2)}, u32[]{:S(2)}) collective-permute-start(bf16[4,64,512]{2,1,0:T(8,128)(2,1)S(1)} %shard_map.51.refs_0_), channel_id=1, source_target_pairs={{0,4},{1,5},{2,6},{3,7},{4,8},{5,9},{6,10},{7,11},{8,12},{9,13},{1... | collective-permute-start | bytes 786440 | tf_op jit(solution)/shard_map/ppermute | solution.py:45
  74.9 23.2 %collective-permute-start.10 = (bf16[4,64,512]{2,1,0:T(8,128)(2,1)S(1)}, bf16[4,64,512]{2,1,0:T(8,128)(2,1)S(1)}, u32[]{:S(2)}, u32[]{:S(2)}) collective-permute-start(bf16[4,64,512]{2,1,0:T(8,128)(2,1)S(1)} %shard_map.51.refs_0_), channel_id=1, source_target_pairs={{0,8},{1,9},{2,10},{3,11},{4,12},{5,13},{6,14},{7,15},{8,0},{9,1},... | collective-permute-start | bytes 786440 | tf_op jit(solution)/shard_map/ppermute | solution.py:45
  77.3 20.7 %collective-permute-start.11 = (bf16[4,64,512]{2,1,0:T(8,128)(2,1)S(1)}, bf16[4,64,512]{2,1,0:T(8,128)(2,1)S(1)}, u32[]{:S(2)}, u32[]{:S(2)}) collective-permute-start(bf16[4,64,512]{2,1,0:T(8,128)(2,1)S(1)} %shard_map.51.refs_0_), channel_id=1, source_target_pairs={{0,12},{1,13},{2,14},{3,15},{4,0},{5,1},{6,2},{7,3},{8,4},{9,5},{1... | collective-permute-start | bytes 786440 | tf_op jit(solution)/shard_map/ppermute | solution.py:45
  81.2 2.2 %copy-start.1 = (bf16[2,16,64,1024]{3,2,1,0:T(8,128)(2,1)S(1)}, bf16[2,16,64,1024]{3,2,1,0:T(8,128)(2,1)}, u32[]{:S(2)}) copy-start(bf16[2,16,64,1024]{3,2,1,0:T(8,128)(2,1)} %copy-done) | copy-start | bytes 12582916
  84.3 0.7 collective-permute-start.7
  97.1 1.6 copy-start.7
  98.1 3.2 %collective-permute-start.13 = (bf16[16,1,64,512]{3,2,1,0:T(8,128)(2,1)}, bf16[16,1,64,512]{3,2,1,0:T(8,128)(2,1)S(1)}, u32[]{:S(2)}, u32[]{:S(2)}) collective-permute-start(bf16[16,1,64,512]{3,2,1,0:T(8,128)(2,1)} %collective-permute-done.8.refs_0_), channel_id=1, source_target_pairs={{0,16},{16,0},{1,17},{17,1},{2,18},{18,2},{3,19},{19,3},{4,20},{20... | collective-permute-start | bytes 3145736 | tf_op jit(solution)/shard_map/ppermute | solution.py:39
  98.7 3.8 %collective-permute-start.14 = (bf16[16,1,64,512]{3,2,1,0:T(8,128)(2,1)S(1)}, bf16[16,1,64,512]{3,2,1,0:T(8,128)(2,1)S(1)}, u32[]{:S(2)}, u32[]{:S(2)}) collective-permute-start(bf16[16,1,64,512]{3,2,1,0:T(8,128)(2,1)S(1)} %copy-done.7), channel_id=1, source_target_pairs={{0,16},{16,0},{1,17},{17,1},{2,18},{18,2},{3,19},{19,3},{4,20},{20... | collective-permute-start | bytes 3145736 | tf_op jit(solution)/shard_map/ppermute | solution.py:39
  99.0 23.2 %collective-permute-start.16 = (bf16[16,64,512]{2,1,0:T(8,128)(2,1)S(1)}, bf16[16,64,512]{2,1,0:T(8,128)(2,1)S(1)}, u32[]{:S(2)}, u32[]{:S(2)}) collective-permute-start(bf16[16,64,512]{2,1,0:T(8,128)(2,1)S(1)} %shard_map.62.inverse_own_ref), channel_id=1, source_target_pairs={{0,16},{16,0},{1,17},{17,1},{2,18},{18,2},{3,19},{19,3},{4,20},{20... | collective-permute-start | bytes 3145736 | tf_op jit(solution)/shard_map/ppermute | solution.py:39
  99.4 6.5 %collective-permute-start.12 = (f32[32,1024]{1,0:T(8,128)S(1)}, f32[32,1024]{1,0:T(8,128)S(1)}, u32[]{:S(2)}, u32[]{:S(2)}) collective-permute-start(f32[32,1024]{1,0:T(8,128)S(1)} %shard_map.58.base_ref.state_ref), channel_id=1, source_target_pairs={{160,96},{161,97},{162,98},{163,99},{164,100},{165,101},{166,102},... | collective-permute-start | bytes 393224 | tf_op jit(solution)/shard_map/ppermute | solution.py:35
  101.2 1.3 copy-start.8
  102.5 1.1 copy-start.9
  103.6 3.4 %copy-start.2 = (bf16[2,16,64,1024]{3,2,1,0:T(8,128)(2,1)S(1)}, bf16[2,16,64,1024]{3,2,1,0:T(8,128)(2,1)}, u32[]{:S(2)}) copy-start(bf16[2,16,64,1024]{3,2,1,0:T(8,128)(2,1)} %copy-done) | copy-start | bytes 12582916
  121.6 0.7 collective-permute-start.15
  138.4 24.7 %collective-permute-start.17 = (bf16[32,1024]{1,0:T(8,128)(2,1)S(1)}, bf16[32,1024]{1,0:T(8,128)(2,1)S(1)}, u32[]{:S(2)}, u32[]{:S(2)}) collective-permute-start(bf16[32,1024]{1,0:T(8,128)(2,1)S(1)} %get-tuple-element.42), channel_id=1, source_target_pairs={{32,0},{96,64},{160,128},{192,160},{224,192},{33,1},{97,65},{161,1... | collective-permute-start | bytes 196616 | tf_op jit(solution)/shard_map/ppermute | solution.py:35
  182.3 4.7 %collective-permute-start.18 = (bf16[16,32,1024]{2,1,0:T(8,128)(2,1)S(1)}, bf16[16,32,1024]{2,1,0:T(8,128)(2,1)S(1)}, u32[]{:S(2)}, u32[]{:S(2)}) collective-permute-start(bf16[16,32,1024]{2,1,0:T(8,128)(2,1)S(1)} %all_to_all.39.own_ref), channel_id=1, source_target_pairs={{0,16},{16,0},{1,17},{17,1},{2,18},{18,2},{3,19},{19,3},{4,20},{20... | collective-permute-start | bytes 3145736 | tf_op jit(solution)/shard_map/ppermute | solution.py:39
